TPU v7x, 32 devices: a whole 2x2x4 slice. The times are simulated.
32 devices in a mesh: table: 16 (over z, y, core), rep: 2 (over x).
Axes of the slice: x: 2, y: 2, z: 4, core: 2. Of those that a mesh axis runs over, the one named last changes fastest.
Arguments:
- bag_rows: int32 [32, 1024, 8], P(('table', 'rep')), may hold values from 0 to 2047
- bag_owner: int32 [32, 1024, 8], P(('table', 'rep')), may hold values from 0 to 15, all different within a row; in each aligned block of 1024 rows (0 to 1023, 1024 to 2047, ..., all dimensions but the last counted through in order) at most 768 rows name the same one
- bag_weight: float32 [32, 1024, 8], P(('table', 'rep')), may hold values from 0.25 to 2
- tables: bfloat16 [4, 32768, 128], P(None, 'table'), may hold values from -3 to 3
- returning: int32 [32], P(('table', 'rep')), may hold values 0 or 1
- home: int32 [32], P(('table', 'rep')), may hold values from 0 to 1
- entry: int32 [32], P(('table', 'rep')), may hold values from 0 to 7
- stores: bfloat16 [256, 30, 512], P(('table', 'rep')), may hold values from -6 to 6
- conv_weight: bfloat16 [4, 1536, 512], P(None, 'table'), may hold values from -0.15625 to 0.15625
- norm_gain: float32 [4, 512], replicated, may hold values from 0.1 to 1.9
Outputs:
- hidden: bfloat16 [32, 1024, 512], P(('table', 'rep'))
Inputs may be any that keep to these rules, and one draw needn't show every extreme that they name: `bag_owner`: the 8 ids of one slot name different owners. Among the slots of one device no owner is named by more than 768 ids, and in some devices' slots one owner is named by exactly 768.
All inputs are finite; a program needn't handle non-finite values. No bound on the sum of `returning` on one device may be relied on, other than what follows from the above.
Results may differ from a plain program's by a relative error of at most 0.0057.
Values may be sent and summed in bfloat16 or wider, within the bound.
No kernel may reach another device: no remote copies, remote signals or barrier semaphores. Data moves between devices by JAX's collectives and lax.ppermute only.
A program may use at most 64 MiB of HBM per device.

v0:
```python
import functools
import jax
import jax.numpy as jnp
from jax import lax
from jax.experimental import pallas as pl
from jax.experimental.pallas import tpu as pltpu
from jax.sharding import PartitionSpec as P

table_of_id = (0, 1, 2, 2, 3, 3, 3, 3)
bag_bounds = ((0, 1), (1, 2), (2, 4), (4, 8))
epsilon = 1e-05
part_ends = (0.25, 2 / 3, 1.0)
stage_parts = (2, 3)
megabyte = 1024 * 1024


def prep_kernel(cuts, shard_rows, rows_ref, owner_ref, request_ref, place_ref):
    owner = owner_ref[...]
    rows = rows_ref[...]
    owners = request_ref.shape[0]
    width, slots = owner.shape
    value_bits = (len(bag_bounds) * shard_rows).bit_length()
    owner_ids = lax.broadcasted_iota(jnp.int32, (owners, slots), 0)
    lane = lax.broadcasted_iota(jnp.int32, (owners, slots), 1)
    value = jnp.zeros((owners, slots), jnp.int32)
    for k in range(width):
        named = owner[k : k + 1, :] == owner_ids
        value = jnp.where(named, rows[k : k + 1, :] + (table_of_id[k] * shard_rows + 1), value)
    present = jnp.where(value > 0, 1, 0)
    rank = present
    step = 1
    while step < slots:
        rank = rank + jnp.where(lane >= step, pltpu.roll(rank, step, 1), 0)
        step *= 2
    rank = rank - present
    place = jnp.zeros((width, slots), jnp.int32)
    for number in range(owners):
        place = jnp.where(owner == number, rank[number : number + 1, :], place)
    landing = jnp.zeros((width, slots), jnp.int32)
    for start, stop in zip(cuts[:-1], cuts[1:]):
        where = owners * start + owner * (stop - start) + place - start
        landing = jnp.where(place >= start, where, landing)
    place_ref[...] = landing
    packed = jnp.where(value > 0, ((lane - rank) << value_bits) + value, 0)
    step = 1
    level = value_bits
    while step < slots:
        moving = jnp.where(((packed >> level) & 1) == 1, packed, 0)
        packed = (packed - moving) + pltpu.roll(moving, slots - step, 1)
        step *= 2
        level += 1
    value = jnp.maximum((packed & ((1 << value_bits) - 1)) - 1, 0)
    for number in range(owners):
        request_ref[number] = value[number : number + 1, : request_ref.shape[2]]


def pass_kernel(*refs):
    pass


def tie(array, *others):
    anywhere = pl.BlockSpec(memory_space=pl.ANY)
    return pl.pallas_call(
        pass_kernel,
        out_shape=jax.ShapeDtypeStruct(array.shape, array.dtype),
        in_specs=[anywhere] * (1 + len(others)),
        out_specs=anywhere,
        input_output_aliases={0: 0},
        name="tie",
    )(array, *others)


def gather_kernel(capacity, first, index_ref, table_ref, *refs):
    out_ref, narrow, wide, picked, packed, index, index_sem, table_sems, out_sems = refs[-9:]
    owners, piece, _ = out_ref.shape
    unroll = 32 if piece % 32 == 0 else 16
    blocks = table_sems.shape[0]
    block_rows = table_ref.shape[0] // blocks
    table_copies = []
    for block in range(blocks):
        part = pl.ds(block * block_rows, block_rows)
        copy = pltpu.make_async_copy(table_ref.at[part, :], narrow.at[part, :], table_sems.at[block])
        copy.start()
        table_copies.append(copy)
    index_copy = pltpu.make_async_copy(index_ref, index, index_sem)
    index_copy.start()
    rows = 256

    for block in range(blocks):
        table_copies[block].wait()

        def widen(step, carry, block=block):
            base = pl.multiple_of(block * block_rows + step * rows, rows)
            wide[pl.ds(base, rows), :] = narrow[pl.ds(base, rows), :].astype(jnp.float32)
            return carry

        lax.fori_loop(0, block_rows // rows, widen, 0)
    index_copy.wait()
    copies = []
    for number in range(owners):
        origin = number * capacity + first

        def some_rows(block, carry, origin=origin):
            base = pl.multiple_of(block * unroll, unroll)
            picks = [index[origin + base + i] for i in range(unroll)]
            found = [wide[pl.ds(pick, 1), :] for pick in picks]
            for i in range(unroll):
                picked[pl.ds(base + i, 1), :] = found[i]
            return carry

        lax.fori_loop(0, piece // unroll, some_rows, 0)
        packed[number] = picked[...].astype(jnp.bfloat16)
        copy = pltpu.make_async_copy(packed.at[number], out_ref.at[number], out_sems.at[number])
        copy.start()
        copies.append(copy)
    for copy in copies:
        copy.wait()


def stage_kernel(
    pieces, first, aliased, place_ref, weight_ref, carried_ref, gain_ref, filter_ref, *refs
):
    piece_refs = refs[:pieces]
    refs = refs[pieces + aliased :]
    out_ref, state_ref, table, picked, filters, first_buf, second_buf, result = refs[:8]
    filter_sems, out_sems = refs[8:]
    width, slots, lanes = picked.shape
    layers = filter_ref.shape[0]
    filter_copies = []
    for layer in range(layers):
        copy = pltpu.make_async_copy(filter_ref.at[layer], filters.at[layer], filter_sems.at[layer])
        copy.start()
        filter_copies.append(copy)
    start = 0
    for piece_ref in piece_refs:
        count = piece_ref.shape[0]
        rows = 256

        def widen(step, carry, piece_ref=piece_ref, start=start):
            base = pl.multiple_of(step * rows, rows)
            table[pl.ds(start + base, rows), :] = piece_ref[pl.ds(base, rows), :].astype(jnp.float32)
            return carry

        lax.fori_loop(0, count // rows, widen, 0)
        start += count

    def some_slots(step, carry):
        base = pl.multiple_of(step * 8, 8)
        for k in range(width):
            picks = [place_ref[k, first + base + i] for i in range(8)]
            rows = [table[pl.ds(pick, 1), :] for pick in picks]
            for i in range(8):
                picked[k, pl.ds(base + i, 1), :] = rows[i]
        return carry

    lax.fori_loop(0, slots // 8, some_slots, 0)
    front = 16
    weights = jnp.transpose(weight_ref[:, first : first + slots])
    for t, (lower, upper) in enumerate(bag_bounds):
        total = picked[lower] * weights[:, lower : lower + 1]
        for k in range(lower + 1, upper):
            total = total + picked[k] * weights[:, k : k + 1]
        total = total.astype(jnp.bfloat16).astype(jnp.float32)
        first_buf[front:, t * lanes : (t + 1) * lanes] = total

    offset = 0
    out_copies = []
    for layer in range(layers):
        dilation = 2**layer
        span = 2 * dilation
        source, target = (first_buf, second_buf) if layer % 2 == 0 else (second_buf, first_buf)
        source[front - span : front, :] = carried_ref[offset : offset + span, :]
        state_ref[offset : offset + span, :] = source[front + slots - span : front + slots, :]
        offset += span
        filter_copies[layer].wait()
        for begin in range(0, slots, 256):
            rows = min(256, slots - begin)
            base = front + begin
            taps = [
                source[base - tap * dilation : base - tap * dilation + rows, :].astype(jnp.bfloat16)
                for tap in range(3)
            ]
            output = jnp.dot(
                jnp.concatenate(taps, axis=1), filters[layer], preferred_element_type=jnp.float32
            )
            mean = jnp.mean(output, axis=-1, keepdims=True)
            centred = output - mean
            spread = jnp.mean(centred * centred, axis=-1, keepdims=True)
            active = jnp.maximum(
                centred * lax.rsqrt(spread + epsilon) * gain_ref[layer : layer + 1, :], 0.0
            )
            if layer % 2 == 1:
                active = active + target[base : base + rows, :]
            active = active.astype(jnp.bfloat16)
            if layer == layers - 1:
                result[begin : begin + rows, :] = active
                copy = pltpu.make_async_copy(
                    result.at[pl.ds(begin, rows), :],
                    out_ref.at[pl.ds(first + begin, rows), :],
                    out_sems.at[len(out_copies)],
                )
                copy.start()
                out_copies.append(copy)
            else:
                target[base : base + rows, :] = active.astype(jnp.float32)
    for copy in out_copies:
        copy.wait()


def gather_filters(conv_weight, after_first, after_second):
    owners = lax.axis_size("table")
    copies = lax.axis_size("rep")
    layers, depth, channels = conv_weight.shape
    if owners % 2 or copies % 2 or layers % 2:
        return lax.all_gather(conv_weight, "table", axis=1, tiled=True)
    half = layers // 2
    parity = lax.axis_index("table") % 2
    side = lax.axis_index("rep") % 2
    groups = [list(range(start, owners, 2)) for start in range(2)]
    mine = lax.dynamic_slice_in_dim(conv_weight, side * half, half, 0)
    mine = lax.all_gather(mine, "table", axis_index_groups=groups, axis=0, tiled=False)
    mine = tie(mine, after_first)
    other = lax.ppermute(mine, "rep", [(r, r ^ 1) for r in range(copies)])
    low = jnp.where(side == 0, mine, other)
    high = jnp.where(side == 0, other, mine)
    own = jnp.concatenate([low, high], axis=1)
    own = tie(own, after_second)
    partner = lax.ppermute(own, "table", [(i, i ^ 1) for i in range(owners)])
    even = jnp.where(parity == 0, own, partner)
    odd = jnp.where(parity == 0, partner, own)
    both = jnp.stack([even, odd], axis=1)
    return jnp.transpose(both, (2, 0, 1, 3, 4)).reshape(layers, owners * depth, channels)


def local(
    bag_rows, bag_owner, bag_weight, tables, returning, home, entry, stores, conv_weight, norm_gain
):
    owners = lax.axis_size("table")
    copies = lax.axis_size("rep")
    samples_here, slot_count, bag_width = bag_rows.shape
    token_count = samples_here * slot_count
    shard_rows = tables.shape[1]
    row_width = tables.shape[2]
    channels = conv_weight.shape[-1]
    capacity = min(token_count, (3 * token_count * bag_width + 2 * owners - 1) // (2 * owners))
    cuts = [0] + [round(capacity * end) // 16 * 16 for end in part_ends]
    slot_cuts = [0] + [cuts[part] for part in stage_parts[:-1]] + [token_count]
    smem = pl.BlockSpec(memory_space=pltpu.SMEM)
    vmem = pl.BlockSpec(memory_space=pltpu.VMEM)
    anywhere = pl.BlockSpec(memory_space=pl.ANY)

    rows_by_slot = bag_rows.reshape(token_count, bag_width).T
    owner_by_slot = bag_owner.reshape(token_count, bag_width).T
    requests, place = pl.pallas_call(
        functools.partial(prep_kernel, cuts, shard_rows),
        out_shape=(
            jax.ShapeDtypeStruct((owners, 1, capacity), jnp.int32),
            jax.ShapeDtypeStruct((bag_width, token_count), jnp.int32),
        ),
        in_specs=[vmem, vmem],
        out_specs=(vmem, vmem),
        compiler_params=pltpu.CompilerParams(vmem_limit_bytes=8 * megabyte),
        name="prep",
    )(rows_by_slot, owner_by_slot)
    received = lax.all_to_all(requests, "table", split_axis=0, concat_axis=0, tiled=True)
    received = received.reshape(owners * capacity)
    flat_table = tables.reshape(-1, row_width)
    returned = []
    sent = []
    for number in range(len(part_ends)):
        piece = cuts[number + 1] - cuts[number]
        sent.append(
            pl.pallas_call(
                functools.partial(gather_kernel, capacity, cuts[number]),
                out_shape=jax.ShapeDtypeStruct((owners, piece, row_width), jnp.bfloat16),
                in_specs=[anywhere] * (2 + len(sent[-1:])),
                out_specs=anywhere,
                scratch_shapes=[
                    pltpu.VMEM(flat_table.shape, jnp.bfloat16),
                    pltpu.VMEM(flat_table.shape, jnp.float32),
                    pltpu.VMEM((piece, row_width), jnp.float32),
                    pltpu.VMEM((owners, piece, row_width), jnp.bfloat16),
                    pltpu.SMEM((owners * capacity,), jnp.int32),
                    pltpu.SemaphoreType.DMA,
                    pltpu.SemaphoreType.DMA((8,)),
                    pltpu.SemaphoreType.DMA((owners,)),
                ],
                compiler_params=pltpu.CompilerParams(vmem_limit_bytes=58 * megabyte),
                cost_estimate=pl.CostEstimate(
                    flops=0, bytes_accessed=20 * megabyte, transcendentals=0
                ),
                name="owner_gather",
            )(received, flat_table, *sent[-1:])
        )
        arrived = lax.all_to_all(sent[-1], "table", split_axis=0, concat_axis=0, tiled=True)
        returned.append(arrived.reshape(owners * piece, row_width))
    filters = gather_filters(conv_weight, returned[0], returned[1])

    me = lax.axis_index("rep")
    carried = jnp.zeros(stores.shape[1:], stores.dtype)
    for shift in range(copies):
        arrived = stores
        if shift:
            pairs = [(source, (source + shift) % copies) for source in range(copies)]
            arrived = lax.ppermute(tie(stores, sent[0]), "rep", pairs)
        wanted = (returning[0] > 0) & (home[0] == (me + copies - shift) % copies)
        chosen = lax.dynamic_index_in_dim(arrived, entry[0], 0, keepdims=False)
        carried = jnp.where(wanted, chosen, carried)

    state = carried.astype(jnp.float32)
    weight_by_slot = bag_weight.reshape(token_count, bag_width).T
    hidden = None
    for number, part in enumerate(stage_parts):
        first, last = slot_cuts[number], slot_cuts[number + 1]
        slots = last - first
        known = [] if hidden is None else [hidden]
        pieces = returned[:part]
        hidden, state = pl.pallas_call(
            functools.partial(stage_kernel, part, first, len(known)),
            out_shape=(
                jax.ShapeDtypeStruct((token_count, channels), jnp.bfloat16),
                jax.ShapeDtypeStruct(state.shape, jnp.float32),
            ),
            in_specs=[smem] + [vmem] * 3 + [anywhere] + [vmem] * part + [anywhere] * len(known),
            out_specs=(anywhere, vmem),
            scratch_shapes=[
                pltpu.VMEM((owners * cuts[part], row_width), jnp.float32),
                pltpu.VMEM((bag_width, slots, row_width), jnp.float32),
                pltpu.VMEM(filters.shape, filters.dtype),
                pltpu.VMEM((slots + 16, channels), jnp.float32),
                pltpu.VMEM((slots + 16, channels), jnp.float32),
                pltpu.VMEM((slots, channels), jnp.bfloat16),
                pltpu.SemaphoreType.DMA((filters.shape[0],)),
                pltpu.SemaphoreType.DMA(((slots + 255) // 256,)),
            ],
            input_output_aliases={5 + part: 0} if known else {},
            compiler_params=pltpu.CompilerParams(vmem_limit_bytes=56 * megabyte),
            cost_estimate=pl.CostEstimate(
                flops=2 * slots * 3 * channels * channels * conv_weight.shape[0],
                bytes_accessed=24 * megabyte,
                transcendentals=0,
            ),
            name="stage",
        )(place, weight_by_slot, state, norm_gain, filters, *pieces, *known)
    return hidden.reshape(samples_here, slot_count, channels)


def solution(mesh):
    in_specs = (
        P(("table", "rep"), None, None),
        P(("table", "rep"), None, None),
        P(("table", "rep"), None, None),
        P(None, "table", None),
        P(("table", "rep")),
        P(("table", "rep")),
        P(("table", "rep")),
        P(("table", "rep"), None, None),
        P(None, "table", None),
        P(),
    )
    out_specs = P(("table", "rep"), None, None)
    return jax.shard_map(local, mesh=mesh, in_specs=in_specs, out_specs=out_specs, check_vma=False)
```

profile of v0, /device:TPU:0, one launch (start us, length us, event | category | flops | bytes accessed | tf_op | source)
XLA Modules:
  0.0 180.1 jit_solution(3828099884300840277)
XLA Ops:
  6.5 0.0 copy-start
  6.5 0.0 all-gather.3.cloned.1.call-start
  6.5 1.0 copy-done
  7.5 0.7 constant_dynamic-slice_fusion
  8.2 0.0 all-gather.3.cloned.1.call-update
  8.2 0.0 copy-start.1
  8.3 0.7 copy-done.1
  9.0 0.0 copy-start.2
  9.0 0.8 copy-done.2
  9.8 1.2 prep.1
  11.0 0.0 copy-start.3
  11.0 14.2 %all_to_all.20 = s32[16,1,768]{2,1,0:T(1,128)} all-to-all(s32[16,1,768]{2,1,0:T(1,128)S(1)} %get-tuple-element.11), channel_id=1, replica_groups=mesh['table'=16,'rep'=2] {'table'}, dimensions={0} | all-to-all | bytes 98304 | tf_op jit(solution)/shard_map/all_to_all | solution.py:265
  25.2 0.0 copy-done.3
  25.2 5.4 %owner_gather.3.refs_1_.refs_0_ = bf16[16,192,128]{2,1,0:T(8,128)(2,1)} custom-call(s32[12288]{0:T(1024)} %bitcast.48, bf16[8192,128]{1,0:T(8,128)(2,1)} %bitcast.36), custom_call_target="tpu_custom_call" | custom-call | bytes 20971520 | tf_op jit(solution)/shard_map/owner_gather/pallas_call | solution.py:273
  30.6 3.6 %all-to-all-start.1 = ((bf16[16,192,128]{2,1,0:T(8,128)(2,1)}), bf16[16,192,128]{2,1,0:T(8,128)(2,1)S(1)}, u32[]{:S(2)}, u32[]{:S(2)}) async-start(bf16[16,192,128]{2,1,0:T(8,128)(2,1)} %owner_gather.3.refs_1_.refs_0_), calls=%async_computation.1 | async-start | bytes 1572864 | tf_op jit(solution)/shard_map/all_to_all | solution.py:295
  34.2 7.3 %owner_gather.4.refs_0_ = bf16[16,320,128]{2,1,0:T(8,128)(2,1)} custom-call(s32[12288]{0:T(1024)} %bitcast.49, bf16[8192,128]{1,0:T(8,128)(2,1)} %bitcast.37, bf16[16,192,128]{2,1,0:T(8,128)(2,1)} %owner_gather.3.refs_1_.refs_0_), custom_call_target="tpu_custom_call" | custom-call | bytes 20971520 | tf_op jit(solution)/shard_map/owner_gather/pallas_call | solution.py:273
  41.6 21.1 %all-to-all-done.1 = bf16[16,192,128]{2,1,0:T(8,128)(2,1)S(1)} async-done(((bf16[16,192,128]{2,1,0:T(8,128)(2,1)}), bf16[16,192,128]{2,1,0:T(8,128)(2,1)S(1)}, u32[]{:S(2)}, u32[]{:S(2)}) %all-to-all-start.1) | async-done | bytes 786464 | tf_op jit(solution)/shard_map/all_to_all | solution.py:295
  62.7 0.0 copy-start.6
  62.7 8.2 %all-to-all-start.2 = ((bf16[16,320,128]{2,1,0:T(8,128)(2,1)}), bf16[16,320,128]{2,1,0:T(8,128)(2,1)S(1)}, u32[]{:S(2)}, u32[]{:S(2)}) async-start(bf16[16,320,128]{2,1,0:T(8,128)(2,1)} %owner_gather.4.refs_0_), calls=%async_computation.2 | async-start | bytes 2621440 | tf_op jit(solution)/shard_map/all_to_all | solution.py:295
  70.8 0.0 all-gather.3.cloned.1.call-done
  70.8 0.0 copy-done.6
  70.9 1.6 collective-permute-start.1
  72.4 35.4 %collective-permute-done.1 = bf16[8,2,96,512]{3,2,1,0:T(8,128)(2,1)S(1)} collective-permute-done((bf16[8,2,96,512]{3,2,1,0:T(8,128)(2,1)}, bf16[8,2,96,512]{3,2,1,0:T(8,128)(2,1)S(1)}, u32[]{:S(2)}, u32[]{:S(2)}) %collective-permute-start.1) | collective-permute-done | bytes 1572896 | tf_op jit(solution)/shard_map/ppermute | solution.py:223
  107.9 1.6 broadcast_select_fusion.1
  109.5 2.0 %pad_maximum_fusion.refs_0_ = bf16[8,4,96,512]{3,2,1,0:T(8,128)(2,1)} fusion(bf16[8,2,96,512]{3,2,1,0:T(8,128)(2,1)S(1)} %get-tuple-element.18, bf16[8,2,96,512]{3,2,1,0:T(8,128)(2,1)S(1)} %get-tuple-element.17), kind=kLoop, calls=%fused_computation.1 | loop fusion | flops 1572864 | bytes 6291456 | tf_op jit(solution)/shard_map/concatenate | solution.py:226
  111.5 0.0 all-to-all-done.2
  111.5 0.0 copy-start.5
  111.5 1.1 copy-done.5
  112.5 0.0 collective-permute-start.2
  112.5 6.4 %owner_gather.5 = bf16[16,256,128]{2,1,0:T(8,128)(2,1)} custom-call(s32[12288]{0:T(1024)} %bitcast.50, bf16[8192,128]{1,0:T(8,128)(2,1)} %bitcast.38, bf16[16,320,128]{2,1,0:T(8,128)(2,1)} %owner_gather.4.refs_0_), custom_call_target="tpu_custom_call" | custom-call | bytes 20971520 | tf_op jit(solution)/shard_map/owner_gather/pallas_call | solution.py:273
  118.9 0.0 copy-start.4
  118.9 6.2 %all-to-all-start.3 = ((bf16[16,256,128]{2,1,0:T(8,128)(2,1)}), bf16[16,256,128]{2,1,0:T(8,128)(2,1)}, u32[]{:S(2)}, u32[]{:S(2)}) async-start(bf16[16,256,128]{2,1,0:T(8,128)(2,1)} %owner_gather.5), calls=%async_computation.3 | async-start | bytes 2097152 | tf_op jit(solution)/shard_map/all_to_all | solution.py:295
  125.1 1.0 copy.18
  126.1 0.0 copy-start.7
  126.1 0.7 copy-done.7
  126.8 0.7 copy.21.refs_0_
  127.6 1.5 collective-permute-start
  131.0 5.4 %collective-permute-done = bf16[8,30,512]{2,1,0:T(8,128)(2,1)} collective-permute-done((bf16[8,30,512]{2,1,0:T(8,128)(2,1)}, bf16[8,30,512]{2,1,0:T(8,128)(2,1)}, u32[]{:S(2)}, u32[]{:S(2)}) %collective-permute-start) | collective-permute-done | bytes 245792 | tf_op jit(solution)/shard_map/ppermute | solution.py:305
  136.4 1.4 bitcast_convert_fusion.carried_ref
  137.8 0.0 collective-permute-done.2
  137.8 0.0 copy-done.4
  137.8 2.3 %select_bitcast_fusion.1 = (bf16[8,1,4,96,512]{4,3,2,0,1:T(8,128)(2,1)S(1)}, bf16[8,1,4,96,512]{4,3,2,0,1:T(8,128)(2,1)S(1)}) fusion(bf16[8,4,96,512]{3,2,1,0:T(8,128)(2,1)S(1)} %copy-done.4, bf16[8,4,96,512]{3,2,1,0:T(8,128)(2,1)} %collective-permute-done.2, pred[]{:T(512)S(6)} %eq.21), kind=kLoop, calls=%fused_computation.3 | loop fusion | flops 3145728 | bytes 12582913 | tf_op jit(solution)/shard_map/stack | solution.py:231
  140.1 0.6 maximum_bitcast_fusion
  140.7 3.4 %copy.20 = bf16[4,8,2,96,512]{4,3,2,1,0:T(8,128)(2,1)} copy(bf16[4,8,2,96,512]{4,3,0,1,2:T(8,128)(2,1)S(1)} %maximum_bitcast_fusion) | data formatting | bytes 12582912 | tf_op jit(solution)/shard_map/transpose | solution.py:232
  144.1 14.2 %stage.2 = (bf16[1024,512]{1,0:T(8,128)(2,1)}, f32[30,512]{1,0:T(8,128)}) custom-call(s32[8,1024]{1,0:T(8,128)} %copy-done.3, f32[8,1024]{1,0:T(8,128)} %bitcast.51, f32[30,512]{1,0:T(8,128)} %bitcast_convert_fusion.carried_ref, f32[4,512]{1,0:T(4,128)} %gain_ref.3, bf16[4,1536,512]{2,1,0:T(8,128)(2,1)} %bitcast.39, bf16[3072,128]{1,0:T(8,128)(2,1)} %bitcast.46, ...), custom_call_target="tpu_custom_call" | custom-call | flops 3221225472 | bytes 25165824 | tf_op jit(solution)/shard_map/stage/pallas_call | solution.py:318
  158.4 0.0 all-to-all-done.3
  158.4 14.8 %stage.3 = (bf16[1024,512]{1,0:T(8,128)(2,1)}, f32[30,512]{1,0:T(8,128)}) custom-call(s32[8,1024]{1,0:T(8,128)} %copy-done.3, f32[8,1024]{1,0:T(8,128)} %bitcast.52, f32[30,512]{1,0:T(8,128)} %get-tuple-element.12.carried_ref, f32[4,512]{1,0:T(4,128)} %gain_ref.3, bf16[4,1536,512]{2,1,0:T(8,128)(2,1)} %bitcast.40, ...), custom_call_target="tpu_custom_call", output_to_operand_aliasing={{0}: (8, {})} | custom-call | flops 3221225472 | bytes 25165824 | tf_op jit(solution)/shard_map/stage/pallas_call | solution.py:318
  (3 shorter events, 0.0 us)
Async XLA Ops:
  6.5 1.0 copy-start
  6.5 64.3 %all-gather.3.cloned.1.call-start = ((), (), s32[]{:S(2)}) async-start(), calls=%async_computation.4 | async-start | bytes 1769472 | tf_op jit(solution)/shard_map/all_gather | solution.py:221
  8.2 0.8 copy-start.1
  9.0 0.8 copy-start.2
  11.0 14.2 %copy-start.3 = (s32[8,1024]{1,0:T(8,128)}, s32[8,1024]{1,0:T(8,128)S(1)}, u32[]{:S(2)}) copy-start(s32[8,1024]{1,0:T(8,128)S(1)} %get-tuple-element.10.place_ref) | copy-start | bytes 98308
  30.6 32.1 %all-to-all-start.1 = ((bf16[16,192,128]{2,1,0:T(8,128)(2,1)}), bf16[16,192,128]{2,1,0:T(8,128)(2,1)S(1)}, u32[]{:S(2)}, u32[]{:S(2)}) async-start(bf16[16,192,128]{2,1,0:T(8,128)(2,1)} %owner_gather.3.refs_1_.refs_0_), calls=%async_computation.1 | async-start | bytes 1572864 | tf_op jit(solution)/shard_map/all_to_all | solution.py:295
  62.7 8.2 %copy-start.6 = (bf16[16,192,128]{2,1,0:T(8,128)(2,1)}, bf16[16,192,128]{2,1,0:T(8,128)(2,1)S(1)}, u32[]{:S(2)}) copy-start(bf16[16,192,128]{2,1,0:T(8,128)(2,1)S(1)} %all-to-all-done.1) | copy-start | bytes 2359300
  62.7 48.8 %all-to-all-start.2 = ((bf16[16,320,128]{2,1,0:T(8,128)(2,1)}), bf16[16,320,128]{2,1,0:T(8,128)(2,1)S(1)}, u32[]{:S(2)}, u32[]{:S(2)}) async-start(bf16[16,320,128]{2,1,0:T(8,128)(2,1)} %owner_gather.4.refs_0_), calls=%async_computation.2 | async-start | bytes 2621440 | tf_op jit(solution)/shard_map/all_to_all | solution.py:295
  70.9 37.0 %collective-permute-start.1 = (bf16[8,2,96,512]{3,2,1,0:T(8,128)(2,1)}, bf16[8,2,96,512]{3,2,1,0:T(8,128)(2,1)S(1)}, u32[]{:S(2)}, u32[]{:S(2)}) collective-permute-start(bf16[8,2,96,512]{3,2,1,0:T(8,128)(2,1)} %tie.4), channel_id=1, source_target_pairs={{0,1},{1,0},{2,3},{3,2},{4,5},{5,4},{6,7},{7,6},{8,9},{9,8},{10,11... | collective-permute-start | bytes 4718600 | tf_op jit(solution)/shard_map/ppermute | solution.py:223
  111.5 1.1 copy-start.5
  112.5 25.3 %collective-permute-start.2 = (bf16[8,4,96,512]{3,2,1,0:T(8,128)(2,1)}, bf16[8,4,96,512]{3,2,1,0:T(8,128)(2,1)}, u32[]{:S(2)}, u32[]{:S(2)}) collective-permute-start(bf16[8,4,96,512]{3,2,1,0:T(8,128)(2,1)} %tie.5), channel_id=1, source_target_pairs={{0,2},{2,0},{4,6},{6,4},{8,10},{10,8},{12,14},{14,12},{16,18},{18,... | collective-permute-start | bytes 9437192 | tf_op jit(solution)/shard_map/ppermute | solution.py:228
  118.9 19.0 %copy-start.4 = (bf16[8,4,96,512]{3,2,1,0:T(8,128)(2,1)S(1)}, bf16[8,4,96,512]{3,2,1,0:T(8,128)(2,1)}, u32[]{:S(2)}) copy-start(bf16[8,4,96,512]{3,2,1,0:T(8,128)(2,1)} %tie.5) | copy-start | bytes 9437188
  118.9 39.5 %all-to-all-start.3 = ((bf16[16,256,128]{2,1,0:T(8,128)(2,1)}), bf16[16,256,128]{2,1,0:T(8,128)(2,1)}, u32[]{:S(2)}, u32[]{:S(2)}) async-start(bf16[16,256,128]{2,1,0:T(8,128)(2,1)} %owner_gather.5), calls=%async_computation.3 | async-start | bytes 2097152 | tf_op jit(solution)/shard_map/all_to_all | solution.py:295
  126.1 0.7 copy-start.7
  127.6 8.9 %collective-permute-start = (bf16[8,30,512]{2,1,0:T(8,128)(2,1)}, bf16[8,30,512]{2,1,0:T(8,128)(2,1)}, u32[]{:S(2)}, u32[]{:S(2)}) collective-permute-start(bf16[8,30,512]{2,1,0:T(8,128)(2,1)} %tie.3), channel_id=1, source_target_pairs={{0,1},{1,0},{2,3},{3,2},{4,5},{5,4},{6,7},{7,6},{8,9},{9,8},{10,11... | collective-permute-start | bytes 737288 | tf_op jit(solution)/shard_map/ppermute | solution.py:305
Sparse Core Ops, SparseCore 0:
  9.5 57.5 all-gather.2
where the time goes:
time: 181 us; the launch traced here: 180 us
  waiting for transfers between devices  62 us (34%)
  Pallas kernels  49.4 us (27%)
  starting transfers between devices  21 us (12%)
  between operations  15.5 us (9%)
  blocking collectives  14.2 us (8%)
  local copies, waits for them, and re-layouts  10.1 us (6%)
  other arithmetic  7.87 us (4%)
    ppermute x1, waiting for transfers between devices, gather_filters(): other = lax.ppermute(mine, 'rep', [(r, r ^ 1) for r in range(copies)])  35.4 us
    pallas_call x2, Pallas kernels, local(): pl.pallas_call(functools.partial(stage_kernel, part, first, len(known)),...  29.1 us
    all_to_all x3, waiting for transfers between devices, local(): lax.all_to_all(sent[-1], 'table', split_axis=0, concat_axis=0, tiled=True)  21.1 us
    pallas_call x3, Pallas kernels, local(): pl.pallas_call(functools.partial(gather_kernel, capacity, cuts[number]),...  19.1 us
    all_to_all x3, starting transfers between devices, local(): lax.all_to_all(sent[-1], 'table', split_axis=0, concat_axis=0, tiled=True)  18 us
    all_to_all x1, blocking collectives, local(): lax.all_to_all(requests, 'table', split_axis=0, concat_axis=0, tiled=True)  14.2 us
    unnamed x18, local copies, waits for them, and re-layouts  6.03 us
    ppermute x1, waiting for transfers between devices, local(): arrived = lax.ppermute(tie(stores, sent[0]), 'rep', pairs)  5.41 us
  transfers between devices with their start and end apart: 7, of which 3 were waited for; matrix products, arithmetic and copies ran while one was open for 7% of the time, Pallas kernels for 19%

commit v1 on v0

--- a/solution.py
+++ b/solution.py
@@ -207,36 +207,27 @@
         copy.wait()
 
 
-def gather_filters(conv_weight, after_first, after_second):
-    owners = lax.axis_size("table")
+def carried_rows(returning, home, entry, stores):
     copies = lax.axis_size("rep")
-    layers, depth, channels = conv_weight.shape
-    if owners % 2 or copies % 2 or layers % 2:
-        return lax.all_gather(conv_weight, "table", axis=1, tiled=True)
-    half = layers // 2
-    parity = lax.axis_index("table") % 2
-    side = lax.axis_index("rep") % 2
-    groups = [list(range(start, owners, 2)) for start in range(2)]
-    mine = lax.dynamic_slice_in_dim(conv_weight, side * half, half, 0)
-    mine = lax.all_gather(mine, "table", axis_index_groups=groups, axis=0, tiled=False)
-    mine = tie(mine, after_first)
-    other = lax.ppermute(mine, "rep", [(r, r ^ 1) for r in range(copies)])
-    low = jnp.where(side == 0, mine, other)
-    high = jnp.where(side == 0, other, mine)
-    own = jnp.concatenate([low, high], axis=1)
-    own = tie(own, after_second)
-    partner = lax.ppermute(own, "table", [(i, i ^ 1) for i in range(owners)])
-    even = jnp.where(parity == 0, own, partner)
-    odd = jnp.where(parity == 0, partner, own)
-    both = jnp.stack([even, odd], axis=1)
-    return jnp.transpose(both, (2, 0, 1, 3, 4)).reshape(layers, owners * depth, channels)
+    me = lax.axis_index("rep")
+    by_position = stores.transpose(1, 0, 2)
+    positions, _, channels = by_position.shape
+    carried = jnp.zeros((positions, channels), stores.dtype)
+    for shift in range(copies):
+        arrived = by_position
+        if shift:
+            pairs = [(source, (source + shift) % copies) for source in range(copies)]
+            arrived = lax.ppermute(by_position, "rep", pairs)
+        wanted = (returning[0] > 0) & (home[0] == (me + copies - shift) % copies)
+        chosen = lax.dynamic_index_in_dim(arrived, entry[0], 1, keepdims=False)
+        carried = jnp.where(wanted, chosen, carried)
+    return carried.astype(jnp.float32)
 
 
 def local(
     bag_rows, bag_owner, bag_weight, tables, returning, home, entry, stores, conv_weight, norm_gain
 ):
     owners = lax.axis_size("table")
-    copies = lax.axis_size("rep")
     samples_here, slot_count, bag_width = bag_rows.shape
     token_count = samples_here * slot_count
     shard_rows = tables.shape[1]
@@ -248,6 +239,8 @@
     smem = pl.BlockSpec(memory_space=pltpu.SMEM)
     vmem = pl.BlockSpec(memory_space=pltpu.VMEM)
     anywhere = pl.BlockSpec(memory_space=pl.ANY)
+
+    filters = lax.all_gather(conv_weight, "table", axis=1, tiled=True)
 
     rows_by_slot = bag_rows.reshape(token_count, bag_width).T
     owner_by_slot = bag_owner.reshape(token_count, bag_width).T
@@ -269,11 +262,12 @@
     sent = []
     for number in range(len(part_ends)):
         piece = cuts[number + 1] - cuts[number]
+        earlier = sent[-1:]
         sent.append(
             pl.pallas_call(
                 functools.partial(gather_kernel, capacity, cuts[number]),
                 out_shape=jax.ShapeDtypeStruct((owners, piece, row_width), jnp.bfloat16),
-                in_specs=[anywhere] * (2 + len(sent[-1:])),
+                in_specs=[anywhere] * (2 + len(earlier)),
                 out_specs=anywhere,
                 scratch_shapes=[
                     pltpu.VMEM(flat_table.shape, jnp.bfloat16),
@@ -290,24 +284,14 @@
                     flops=0, bytes_accessed=20 * megabyte, transcendentals=0
                 ),
                 name="owner_gather",
-            )(received, flat_table, *sent[-1:])
+            )(received, flat_table, *earlier)
         )
-        arrived = lax.all_to_all(sent[-1], "table", split_axis=0, concat_axis=0, tiled=True)
-        returned.append(arrived.reshape(owners * piece, row_width))
-    filters = gather_filters(conv_weight, returned[0], returned[1])
-
-    me = lax.axis_index("rep")
-    carried = jnp.zeros(stores.shape[1:], stores.dtype)
-    for shift in range(copies):
-        arrived = stores
-        if shift:
-            pairs = [(source, (source + shift) % copies) for source in range(copies)]
-            arrived = lax.ppermute(tie(stores, sent[0]), "rep", pairs)
-        wanted = (returning[0] > 0) & (home[0] == (me + copies - shift) % copies)
-        chosen = lax.dynamic_index_in_dim(arrived, entry[0], 0, keepdims=False)
-        carried = jnp.where(wanted, chosen, carried)
-
-    state = carried.astype(jnp.float32)
+    for number, rows in enumerate(sent):
+        if number:
+            rows = tie(rows, returned[-1], *sent[number + 1 :])
+        arrived = lax.all_to_all(rows, "table", split_axis=0, concat_axis=0, tiled=True)
+        returned.append(arrived.reshape(-1, row_width))
+    state = carried_rows(returning, home, entry, stores)
     weight_by_slot = bag_weight.reshape(token_count, bag_width).T
     hidden = None
     for number, part in enumerate(stage_parts):
@@ -330,7 +314,7 @@
                 pltpu.VMEM((slots + 16, channels), jnp.float32),
                 pltpu.VMEM((slots + 16, channels), jnp.float32),
                 pltpu.VMEM((slots, channels), jnp.bfloat16),
-                pltpu.SemaphoreType.DMA((filters.shape[0],)),
+                pltpu.SemaphoreType.DMA(filters.shape[:1]),
                 pltpu.SemaphoreType.DMA(((slots + 255) // 256,)),
             ],
             input_output_aliases={5 + part: 0} if known else {},

time: 181 us -> 159 us (0.88)
  blocking collectives: 14.2 us -> 63.9 us
  waiting for transfers between devices: 62 us -> 15.6 us
  starting transfers between devices: 21 us -> 9.16 us
  other arithmetic: 7.87 us -> 0.64 us
  local copies, waits for them, and re-layouts: 10.1 us -> 3.57 us
    all_to_all x0 -> x1, blocking collectives: none -> 49.9 us  [local(): lax.all_to_all(rows, 'table', split_axis=0, concat_axis=0, tiled=True)]
    ppermute x3 -> x1, waiting for transfers between devices: 40.8 us -> 5.09 us  [carried_rows(): arrived = lax.ppermute(by_position, 'rep', pairs)]
    all_to_all x3 -> x2, waiting for transfers between devices: 21.1 us -> 9.77 us  [local(): lax.all_to_all(rows, 'table', split_axis=0, concat_axis=0, tiled=True)]
    all_to_all x3 -> x2, starting transfers between devices: 18 us -> 7.62 us  [local(): lax.all_to_all(rows, 'table', split_axis=0, concat_axis=0, tiled=True)]
    transpose x1 -> x0, local copies, waits for them, and re-layouts: 3.41 us -> none  [gather_filters(): jnp.transpose(both, (2, 0, 1, 3, 4))]
    unnamed x18 -> x13, local copies, waits for them, and re-layouts: 6.03 us -> 3.57 us
    another operation x1 -> x0, other arithmetic: 2.3 us -> none  [gather_filters(): both = jnp.stack([even, odd], axis=1)]
    concatenate x1 -> x0, other arithmetic: 1.96 us -> none  [gather_filters(): own = jnp.concatenate([low, high], axis=1)]
  transfers between devices with their start and end apart: 7 -> 4, of which waited for: 3 -> 2; matrix products, arithmetic and copies ran while one was open for 7% -> 0% of each run, Pallas kernels for 19% -> 22%
where the time goes in v1:
time: 159 us; the launch traced here: 158 us
  blocking collectives  63.9 us (40%)
  Pallas kernels  49.4 us (31%)
  waiting for transfers between devices  15.6 us (10%)
  between operations  15.5 us (10%)
  starting transfers between devices  9.16 us (6%)
  local copies, waits for them, and re-layouts  3.57 us (2%)
    all_to_all x1, blocking collectives, local(): lax.all_to_all(rows, 'table', split_axis=0, concat_axis=0, tiled=True)  49.9 us
    pallas_call x2, Pallas kernels, local(): pl.pallas_call(functools.partial(stage_kernel, part, first, len(known)),...  29.1 us
    pallas_call x3, Pallas kernels, local(): pl.pallas_call(functools.partial(gather_kernel, capacity, cuts[number]),...  19.1 us
    all_to_all x1, blocking collectives, local(): lax.all_to_all(requests, 'table', split_axis=0, concat_axis=0, tiled=True)  14.1 us
    all_to_all x2, waiting for transfers between devices, local(): lax.all_to_all(rows, 'table', split_axis=0, concat_axis=0, tiled=True)  9.77 us
    all_to_all x2, starting transfers between devices, local(): lax.all_to_all(rows, 'table', split_axis=0, concat_axis=0, tiled=True)  7.62 us
    ppermute x1, waiting for transfers between devices, carried_rows(): arrived = lax.ppermute(by_position, 'rep', pairs)  5.09 us
    unnamed x13, local copies, waits for them, and re-layouts  3.57 us
  transfers between devices with their start and end apart: 4, of which 2 were waited for; matrix products, arithmetic and copies ran while one was open for 0% of the time, Pallas kernels for 22%

profile of v1, /device:TPU:0, one launch (start us, length us, event | category | flops | bytes accessed | tf_op | source)
XLA Modules:
  0.0 157.8 jit_solution(5097186773730475031)
XLA Ops:
  6.5 0.0 all-gather.2.cloned.1.call-start
  6.5 0.7 all-gather.2.cloned.1.call-update
  7.3 0.0 copy-start
  7.3 0.7 copy-done
  8.0 0.0 copy-start.1
  8.0 0.8 copy-done.1
  8.8 1.2 prep.1
  10.0 0.0 copy-start.2
  10.0 14.1 %all_to_all.20 = s32[16,1,768]{2,1,0:T(1,128)} all-to-all(s32[16,1,768]{2,1,0:T(1,128)S(1)} %get-tuple-element.11), channel_id=1, replica_groups=mesh['table'=16,'rep'=2] {'table'}, dimensions={0} | all-to-all | bytes 98304 | tf_op jit(solution)/shard_map/all_to_all | solution.py:258
  24.1 0.0 copy-done.2
  24.1 5.4 %owner_gather.3.refs_0_ = bf16[16,192,128]{2,1,0:T(8,128)(2,1)} custom-call(s32[12288]{0:T(1024)} %bitcast.44, bf16[8192,128]{1,0:T(8,128)(2,1)} %bitcast.34), custom_call_target="tpu_custom_call" | custom-call | bytes 20971520 | tf_op jit(solution)/shard_map/owner_gather/pallas_call | solution.py:267
  29.5 3.6 %all-to-all-start.1 = ((bf16[16,192,128]{2,1,0:T(8,128)(2,1)}), bf16[16,192,128]{2,1,0:T(8,128)(2,1)S(1)}, u32[]{:S(2)}, u32[]{:S(2)}) async-start(bf16[16,192,128]{2,1,0:T(8,128)(2,1)} %owner_gather.3.refs_0_), calls=%async_computation.1 | async-start | bytes 1572864 | tf_op jit(solution)/shard_map/all_to_all | solution.py:292
  33.1 7.3 %owner_gather.4.refs_0_ = bf16[16,320,128]{2,1,0:T(8,128)(2,1)} custom-call(s32[12288]{0:T(1024)} %bitcast.45, bf16[8192,128]{1,0:T(8,128)(2,1)} %bitcast.35, bf16[16,192,128]{2,1,0:T(8,128)(2,1)} %owner_gather.3.refs_0_), custom_call_target="tpu_custom_call" | custom-call | bytes 20971520 | tf_op jit(solution)/shard_map/owner_gather/pallas_call | solution.py:267
  40.5 6.4 %owner_gather.5.refs_2_.refs_0_ = bf16[16,256,128]{2,1,0:T(8,128)(2,1)} custom-call(s32[12288]{0:T(1024)} %bitcast.46, bf16[8192,128]{1,0:T(8,128)(2,1)} %bitcast.36, bf16[16,320,128]{2,1,0:T(8,128)(2,1)} %owner_gather.4.refs_0_), custom_call_target="tpu_custom_call" | custom-call | bytes 20971520 | tf_op jit(solution)/shard_map/owner_gather/pallas_call | solution.py:267
  46.9 9.8 %all-to-all-done.1 = bf16[16,192,128]{2,1,0:T(8,128)(2,1)S(1)} async-done(((bf16[16,192,128]{2,1,0:T(8,128)(2,1)}), bf16[16,192,128]{2,1,0:T(8,128)(2,1)S(1)}, u32[]{:S(2)}, u32[]{:S(2)}) %all-to-all-start.1) | async-done | bytes 786464 | tf_op jit(solution)/shard_map/all_to_all | solution.py:292
  56.6 0.0 copy-start.3
  56.6 0.9 copy-done.3
  57.5 49.9 %all_to_all.21 = bf16[16,320,128]{2,1,0:T(8,128)(2,1)} all-to-all(bf16[16,320,128]{2,1,0:T(8,128)(2,1)} %tie.2), channel_id=1, replica_groups=mesh['table'=16,'rep'=2] {'table'}, dimensions={0} | all-to-all | bytes 2621440 | tf_op jit(solution)/shard_map/all_to_all | solution.py:292
  107.4 0.0 copy-start.5
  107.4 4.0 %all-to-all-start.3 = ((bf16[16,256,128]{2,1,0:T(8,128)(2,1)}), bf16[16,256,128]{2,1,0:T(8,128)(2,1)S(1)}, u32[]{:S(2)}, u32[]{:S(2)}) async-start(bf16[16,256,128]{2,1,0:T(8,128)(2,1)} %tie.3), calls=%async_computation.3 | async-start | bytes 2097152 | tf_op jit(solution)/shard_map/all_to_all | solution.py:292
  111.4 0.0 copy-done.5
  111.4 0.1 copy.19
  111.5 1.5 collective-permute-start
  115.0 5.1 %collective-permute-done = bf16[30,8,512]{2,0,1:T(8,128)(2,1)S(1)} collective-permute-done((bf16[30,8,512]{2,0,1:T(8,128)(2,1)S(1)}, bf16[30,8,512]{2,0,1:T(8,128)(2,1)S(1)}, u32[]{:S(2)}, u32[]{:S(2)}) %collective-permute-start) | collective-permute-done | bytes 245792 | tf_op jit(solution)/shard_map/ppermute | solution.py:220
  120.1 0.6 fusion.carried_ref
  120.8 0.0 all-gather.2.cloned.1.call-done.filter_ref
  120.8 14.3 %stage.2 = (bf16[1024,512]{1,0:T(8,128)(2,1)}, f32[30,512]{1,0:T(8,128)}) custom-call(s32[8,1024]{1,0:T(8,128)} %copy-done.2, f32[8,1024]{1,0:T(8,128)} %bitcast.48, f32[30,512]{1,0:T(8,128)} %fusion.carried_ref, f32[4,512]{1,0:T(4,128)} %gain_ref.3, bf16[4,1536,512]{2,1,0:T(8,128)(2,1)} %all-gather.2.cloned.1.call-done.filter_ref, ...), custom_call_target="tpu_custom_call" | custom-call | flops 3221225472 | bytes 25165824 | tf_op jit(solution)/shard_map/stage/pallas_call | solution.py:302
  135.0 0.0 all-to-all-done.3
  135.0 0.0 copy-start.4
  135.0 1.1 copy-done.4
  136.1 14.8 %stage.3 = (bf16[1024,512]{1,0:T(8,128)(2,1)}, f32[30,512]{1,0:T(8,128)}) custom-call(s32[8,1024]{1,0:T(8,128)} %copy-done.2, f32[8,1024]{1,0:T(8,128)} %bitcast.49, f32[30,512]{1,0:T(8,128)} %get-tuple-element.12.carried_ref, f32[4,512]{1,0:T(4,128)} %gain_ref.3, ...), custom_call_target="tpu_custom_call", output_to_operand_aliasing={{0}: (8, {})} | custom-call | flops 3221225472 | bytes 25165824 | tf_op jit(solution)/shard_map/stage/pallas_call | solution.py:302
  (2 shorter events, 0.0 us)
Async XLA Ops:
  6.5 114.2 %all-gather.2.cloned.1.call-start = ((), (), s32[]{:S(2)}) async-start(), calls=%async_computation.4 | async-start | bytes 6684672 | tf_op jit(solution)/shard_map/all_gather | solution.py:243
  7.3 0.8 copy-start
  8.0 0.8 copy-start.1
  10.0 14.1 %copy-start.2 = (s32[8,1024]{1,0:T(8,128)}, s32[8,1024]{1,0:T(8,128)S(1)}, u32[]{:S(2)}) copy-start(s32[8,1024]{1,0:T(8,128)S(1)} %get-tuple-element.10.place_ref) | copy-start | bytes 98308
  29.5 27.1 %all-to-all-start.1 = ((bf16[16,192,128]{2,1,0:T(8,128)(2,1)}), bf16[16,192,128]{2,1,0:T(8,128)(2,1)S(1)}, u32[]{:S(2)}, u32[]{:S(2)}) async-start(bf16[16,192,128]{2,1,0:T(8,128)(2,1)} %owner_gather.3.refs_0_), calls=%async_computation.1 | async-start | bytes 1572864 | tf_op jit(solution)/shard_map/all_to_all | solution.py:292
  56.6 0.9 copy-start.3
  107.4 4.0 %copy-start.5 = (bf16[8,30,512]{2,0,1:T(8,128)(2,1)S(1)}, bf16[8,30,512]{2,0,1:T(8,128)(2,1)}, u32[]{:S(2)}) copy-start(bf16[8,30,512]{2,0,1:T(8,128)(2,1)} %param.17) | copy-start | bytes 737284
  107.4 27.6 %all-to-all-start.3 = ((bf16[16,256,128]{2,1,0:T(8,128)(2,1)}), bf16[16,256,128]{2,1,0:T(8,128)(2,1)S(1)}, u32[]{:S(2)}, u32[]{:S(2)}) async-start(bf16[16,256,128]{2,1,0:T(8,128)(2,1)} %tie.3), calls=%async_computation.3 | async-start | bytes 2097152 | tf_op jit(solution)/shard_map/all_to_all | solution.py:292
  111.5 8.6 %collective-permute-start = (bf16[30,8,512]{2,0,1:T(8,128)(2,1)S(1)}, bf16[30,8,512]{2,0,1:T(8,128)(2,1)S(1)}, u32[]{:S(2)}, u32[]{:S(2)}) collective-permute-start(bf16[30,8,512]{2,0,1:T(8,128)(2,1)S(1)} %bitcast.47), channel_id=1, source_target_pairs={{0,1},{1,0},{2,3},{3,2},{4,5},{5,4},{6,7},{7,6},{8,9},{9,8},{10,11... | collective-permute-start | bytes 737288 | tf_op jit(solution)/shard_map/ppermute | solution.py:220
  135.0 1.1 copy-start.4
Sparse Core Ops, SparseCore 0:
  9.6 82.5 all-gather.1

commit v2 on v1

--- a/solution.py
+++ b/solution.py
@@ -118,19 +118,29 @@
 
 
 def stage_kernel(
-    pieces, first, aliased, place_ref, weight_ref, carried_ref, gain_ref, filter_ref, *refs
+    pieces, sources, first, aliased, place_ref, me_ref, weight_ref, carried_ref, gain_ref, *refs
 ):
     piece_refs = refs[:pieces]
-    refs = refs[pieces + aliased :]
+    filter_refs = refs[pieces : pieces + sources]
+    refs = refs[pieces + sources + aliased :]
     out_ref, state_ref, table, picked, filters, first_buf, second_buf, result = refs[:8]
     filter_sems, out_sems = refs[8:]
     width, slots, lanes = picked.shape
-    layers = filter_ref.shape[0]
+    layers = filters.shape[0]
     filter_copies = []
-    for layer in range(layers):
-        copy = pltpu.make_async_copy(filter_ref.at[layer], filters.at[layer], filter_sems.at[layer])
+    if sources == 1:
+        filter_copies.append(pltpu.make_async_copy(filter_refs[0], filters, filter_sems.at[0]))
+    else:
+        held, _, depth, _ = filter_refs[0].shape
+        for number in range(2 * held):
+            owner = me_ref[0] ^ shard_offset(2 * held, number)
+            rows = pl.ds(pl.multiple_of(owner * depth, depth), depth)
+            source = filter_refs[number // held].at[number % held]
+            filter_copies.append(
+                pltpu.make_async_copy(source, filters.at[:, rows, :], filter_sems.at[number])
+            )
+    for copy in filter_copies:
         copy.start()
-        filter_copies.append(copy)
     start = 0
     for piece_ref in piece_refs:
         count = piece_ref.shape[0]
@@ -163,6 +173,8 @@
         total = total.astype(jnp.bfloat16).astype(jnp.float32)
         first_buf[front:, t * lanes : (t + 1) * lanes] = total
 
+    for copy in filter_copies:
+        copy.wait()
     offset = 0
     out_copies = []
     for layer in range(layers):
@@ -172,7 +184,6 @@
         source[front - span : front, :] = carried_ref[offset : offset + span, :]
         state_ref[offset : offset + span, :] = source[front + slots - span : front + slots, :]
         offset += span
-        filter_copies[layer].wait()
         for begin in range(0, slots, 256):
             rows = min(256, slots - begin)
             base = front + begin
@@ -207,6 +218,23 @@
         copy.wait()
 
 
+def swap_filters(shards, distance, after):
+    owners = lax.axis_size("table")
+    shards = tie(shards, after)
+    pairs = [(source, source ^ distance) for source in range(owners)]
+    return shards, lax.ppermute(shards, "table", pairs)
+
+
+def shard_offset(owners, number):
+    offset = 0
+    bit = owners // 2
+    while bit:
+        offset += bit * (number % 2)
+        number //= 2
+        bit //= 2
+    return offset
+
+
 def carried_rows(returning, home, entry, stores):
     copies = lax.axis_size("rep")
     me = lax.axis_index("rep")
@@ -240,8 +268,7 @@
     vmem = pl.BlockSpec(memory_space=pltpu.VMEM)
     anywhere = pl.BlockSpec(memory_space=pl.ANY)
 
-    filters = lax.all_gather(conv_weight, "table", axis=1, tiled=True)
-
+    me = lax.axis_index("table").astype(jnp.int32).reshape(1)
     rows_by_slot = bag_rows.reshape(token_count, bag_width).T
     owner_by_slot = bag_owner.reshape(token_count, bag_width).T
     requests, place = pl.pallas_call(
@@ -291,6 +318,18 @@
             rows = tie(rows, returned[-1], *sent[number + 1 :])
         arrived = lax.all_to_all(rows, "table", split_axis=0, concat_axis=0, tiled=True)
         returned.append(arrived.reshape(-1, row_width))
+    swaps = owners.bit_length() - 1
+    gates = [place, sent[0]] + [returned[0]] * (swaps - 3) + [returned[1]]
+    filters = [conv_weight[None]]
+    for step in range(swaps):
+        shards = jnp.concatenate(filters, axis=0)
+        filters = list(swap_filters(shards, owners >> (step + 1), gates[step]))
+    if conv_weight.shape[1] % 16:
+        offsets = [shard_offset(owners, number) for number in range(owners)]
+        order = jnp.array([offsets.index(owner) for owner in range(owners)], jnp.int32)
+        sources = order[jnp.arange(owners, dtype=jnp.int32) ^ me]
+        whole = jnp.concatenate(filters, axis=0)[sources]
+        filters = [whole.transpose(1, 0, 2, 3).reshape(conv_weight.shape[0], -1, channels)]
     state = carried_rows(returning, home, entry, stores)
     weight_by_slot = bag_weight.reshape(token_count, bag_width).T
     hidden = None
@@ -300,24 +339,26 @@
         known = [] if hidden is None else [hidden]
         pieces = returned[:part]
         hidden, state = pl.pallas_call(
-            functools.partial(stage_kernel, part, first, len(known)),
+            functools.partial(stage_kernel, part, len(filters), first, len(known)),
             out_shape=(
                 jax.ShapeDtypeStruct((token_count, channels), jnp.bfloat16),
                 jax.ShapeDtypeStruct(state.shape, jnp.float32),
             ),
-            in_specs=[smem] + [vmem] * 3 + [anywhere] + [vmem] * part + [anywhere] * len(known),
+            in_specs=[smem] * 2
+            + [vmem] * (3 + part)
+            + [anywhere] * (len(filters) + len(known)),
             out_specs=(anywhere, vmem),
             scratch_shapes=[
                 pltpu.VMEM((owners * cuts[part], row_width), jnp.float32),
                 pltpu.VMEM((bag_width, slots, row_width), jnp.float32),
-                pltpu.VMEM(filters.shape, filters.dtype),
+                pltpu.VMEM((conv_weight.shape[0], 3 * channels, channels), jnp.bfloat16),
                 pltpu.VMEM((slots + 16, channels), jnp.float32),
                 pltpu.VMEM((slots + 16, channels), jnp.float32),
                 pltpu.VMEM((slots, channels), jnp.bfloat16),
-                pltpu.SemaphoreType.DMA(filters.shape[:1]),
+                pltpu.SemaphoreType.DMA((owners,)),
                 pltpu.SemaphoreType.DMA(((slots + 255) // 256,)),
             ],
-            input_output_aliases={5 + part: 0} if known else {},
+            input_output_aliases={5 + part + len(filters): 0} if known else {},
             compiler_params=pltpu.CompilerParams(vmem_limit_bytes=56 * megabyte),
             cost_estimate=pl.CostEstimate(
                 flops=2 * slots * 3 * channels * channels * conv_weight.shape[0],
@@ -325,7 +366,7 @@
                 transcendentals=0,
             ),
             name="stage",
-        )(place, weight_by_slot, state, norm_gain, filters, *pieces, *known)
+        )(place, me, weight_by_slot, state, norm_gain, *pieces, *filters, *known)
     return hidden.reshape(samples_here, slot_count, channels)
 
 

time: 159 us -> 187 us (1.18)
  waiting for transfers between devices: 15.6 us -> 87.1 us
  blocking collectives: 63.9 us -> 14.1 us
  between operations: 15.5 us -> 2.26 us
  starting transfers between devices: 9.16 us -> 19 us
  other arithmetic: 0.64 us -> 8.38 us
  local copies, waits for them, and re-layouts: 3.57 us -> 6.45 us
  Pallas kernels: 49.4 us -> 47.4 us
    ppermute x0 -> x4, waiting for transfers between devices: none -> 81.7 us  [swap_filters(): return (shards, lax.ppermute(shards, 'table', pairs))]
    all_to_all x1 -> x0, blocking collectives: 49.9 us -> none  [local(): lax.all_to_all(rows, 'table', split_axis=0, concat_axis=0, tiled=True)]
    all_to_all x2 -> x3, waiting for transfers between devices: 9.77 us -> 0.25 us  [local(): lax.all_to_all(rows, 'table', split_axis=0, concat_axis=0, tiled=True)]
    concatenate x0 -> x3, other arithmetic: none -> 7.75 us  [local(): shards = jnp.concatenate(filters, axis=0)]
    all_to_all x2 -> x3, starting transfers between devices: 7.62 us -> 13 us  [local(): lax.all_to_all(rows, 'table', split_axis=0, concat_axis=0, tiled=True)]
    ppermute x0 -> x4, starting transfers between devices: none -> 4.48 us  [swap_filters(): return (shards, lax.ppermute(shards, 'table', pairs))]
    unnamed x13 -> x18, local copies, waits for them, and re-layouts: 3.57 us -> 6.45 us
    pallas_call x2, Pallas kernels: 29.1 us -> 27.1 us  [local(): pl.pallas_call(functools.partial(stage_kernel, part, len(filters), first,...]
  transfers between devices with their start and end apart: 4 -> 8, of which waited for: 2 -> 5; matrix products, arithmetic and copies ran while one was open for 0% -> 5% of each run, Pallas kernels for 22% -> 15%
where the time goes in v2:
time: 187 us; the launch traced here: 185 us
  waiting for transfers between devices  87.1 us (47%)
  Pallas kernels  47.4 us (25%)
  starting transfers between devices  19 us (10%)
  blocking collectives  14.1 us (8%)
  other arithmetic  8.38 us (4%)
  local copies, waits for them, and re-layouts  6.45 us (3%)
  between operations  2.26 us (1%)
    ppermute x4, waiting for transfers between devices, swap_filters(): return (shards, lax.ppermute(shards, 'table', pairs))  81.7 us
    pallas_call x2, Pallas kernels, local(): pl.pallas_call(functools.partial(stage_kernel, part, len(filters), first,...  27.1 us
    pallas_call x3, Pallas kernels, local(): pl.pallas_call(functools.partial(gather_kernel, capacity, cuts[number]),...  19.1 us
    all_to_all x1, blocking collectives, local(): lax.all_to_all(requests, 'table', split_axis=0, concat_axis=0, tiled=True)  14.1 us
    all_to_all x3, starting transfers between devices, local(): lax.all_to_all(rows, 'table', split_axis=0, concat_axis=0, tiled=True)  13 us
    concatenate x3, other arithmetic, local(): shards = jnp.concatenate(filters, axis=0)  7.75 us
    unnamed x18, local copies, waits for them, and re-layouts  6.45 us
    ppermute x1, waiting for transfers between devices, carried_rows(): arrived = lax.ppermute(by_position, 'rep', pairs)  5.18 us
  transfers between devices with their start and end apart: 8, of which 5 were waited for; matrix products, arithmetic and copies ran while one was open for 5% of the time, Pallas kernels for 15%

profile of v2, /device:TPU:0, one launch (start us, length us, event | category | flops | bytes accessed | tf_op | source)
XLA Modules:
  0.0 184.6 jit_solution(4697477513079032693)
XLA Ops:
  0.0 1.8 copy.35
  1.8 0.0 copy-start.1
  1.8 0.8 copy-done.1
  2.5 0.0 copy-start.2
  2.5 0.8 copy-done.2
  3.3 1.2 prep.1
  4.5 0.0 copy-start
  4.6 14.1 %all_to_all.20 = s32[16,1,768]{2,1,0:T(1,128)} all-to-all(s32[16,1,768]{2,1,0:T(1,128)S(1)} %get-tuple-element.11), channel_id=1, replica_groups=mesh['table'=16,'rep'=2] {'table'}, dimensions={0} | all-to-all | bytes 98304 | tf_op jit(solution)/shard_map/all_to_all | solution.py:285
  18.6 0.0 copy-done
  18.6 5.4 %owner_gather.3.refs_0_.refs_1_ = bf16[16,192,128]{2,1,0:T(8,128)(2,1)} custom-call(s32[12288]{0:T(1024)} %bitcast.49, bf16[8192,128]{1,0:T(8,128)(2,1)} %bitcast.36), custom_call_target="tpu_custom_call" | custom-call | bytes 20971520 | tf_op jit(solution)/shard_map/owner_gather/pallas_call | solution.py:294
  24.0 3.6 %all-to-all-start.1 = ((bf16[16,192,128]{2,1,0:T(8,128)(2,1)}), bf16[16,192,128]{2,1,0:T(8,128)(2,1)S(1)}, u32[]{:S(2)}, u32[]{:S(2)}) async-start(bf16[16,192,128]{2,1,0:T(8,128)(2,1)} %owner_gather.3.refs_0_.refs_1_), calls=%async_computation.1 | async-start | bytes 1572864 | tf_op jit(solution)/shard_map/all_to_all | solution.py:319
  27.7 2.8 %collective-permute-start.1 = (bf16[1,4,96,512]{3,2,1,0:T(8,128)(2,1)}, bf16[1,4,96,512]{3,2,1,0:T(8,128)(2,1)S(1)}, u32[]{:S(2)}, u32[]{:S(2)}) collective-permute-start(bf16[1,4,96,512]{3,2,1,0:T(8,128)(2,1)} %tie.7), channel_id=1, source_target_pairs={{0,16},{2,18},{4,20},{6,22},{8,24},{10,26},{12,28},{14,30},{16,0},... | collective-permute-start | bytes 1179656 | tf_op jit(solution)/shard_map/ppermute | solution.py:225
  30.5 34.9 %collective-permute-done.1 = bf16[1,4,96,512]{3,2,1,0:T(8,128)(2,1)S(1)} collective-permute-done((bf16[1,4,96,512]{3,2,1,0:T(8,128)(2,1)}, bf16[1,4,96,512]{3,2,1,0:T(8,128)(2,1)S(1)}, u32[]{:S(2)}, u32[]{:S(2)}) %collective-permute-start.1) | collective-permute-done | bytes 393248 | tf_op jit(solution)/shard_map/ppermute | solution.py:225
  65.4 1.9 %pad_maximum_fusion.2.refs_0_ = bf16[2,4,96,512]{3,2,1,0:T(8,128)(2,1)} fusion(bf16[1,4,96,512]{3,2,1,0:T(8,128)(2,1)S(1)} %collective-permute-done.1, bf16[1,4,96,512]{3,2,1,0:T(8,128)(2,1)} %tie.7), kind=kLoop, calls=%fused_computation.2 | loop fusion | flops 393216 | bytes 1572864 | tf_op jit(solution)/shard_map/concatenate | solution.py:325
  67.3 0.0 collective-permute-start.2
  67.3 7.3 %owner_gather.4.refs_0_ = bf16[16,320,128]{2,1,0:T(8,128)(2,1)} custom-call(s32[12288]{0:T(1024)} %bitcast.50, bf16[8192,128]{1,0:T(8,128)(2,1)} %bitcast.37, bf16[16,192,128]{2,1,0:T(8,128)(2,1)} %owner_gather.3.refs_0_.refs_1_), custom_call_target="tpu_custom_call" | custom-call | bytes 20971520 | tf_op jit(solution)/shard_map/owner_gather/pallas_call | solution.py:294
  74.6 6.4 %owner_gather.5.refs_2_.refs_0_ = bf16[16,256,128]{2,1,0:T(8,128)(2,1)} custom-call(s32[12288]{0:T(1024)} %bitcast.51, bf16[8192,128]{1,0:T(8,128)(2,1)} %bitcast.38, bf16[16,320,128]{2,1,0:T(8,128)(2,1)} %owner_gather.4.refs_0_), custom_call_target="tpu_custom_call" | custom-call | bytes 20971520 | tf_op jit(solution)/shard_map/owner_gather/pallas_call | solution.py:294
  81.0 0.0 all-to-all-done.1
  81.0 0.0 copy-start.5
  81.0 0.9 copy-done.5
  82.0 0.0 copy-start.4
  82.0 4.4 %all-to-all-start.2 = ((bf16[16,320,128]{2,1,0:T(8,128)(2,1)}), bf16[16,320,128]{2,1,0:T(8,128)(2,1)S(1)}, u32[]{:S(2)}, u32[]{:S(2)}) async-start(bf16[16,320,128]{2,1,0:T(8,128)(2,1)} %tie.6), calls=%async_computation.2 | async-start | bytes 2621440 | tf_op jit(solution)/shard_map/all_to_all | solution.py:319
  86.4 0.3 collective-permute-done.2
  86.7 0.0 copy-done.4
  86.7 2.4 %pad_maximum_fusion.1.refs_0_ = bf16[4,4,96,512]{3,2,1,0:T(8,128)(2,1)} fusion(bf16[2,4,96,512]{3,2,1,0:T(8,128)(2,1)} %collective-permute-done.2, bf16[2,4,96,512]{3,2,1,0:T(8,128)(2,1)S(1)} %copy-done.4), kind=kLoop, calls=%fused_computation.1 | loop fusion | flops 786432 | bytes 3145728 | tf_op jit(solution)/shard_map/concatenate | solution.py:325
  89.1 1.7 collective-permute-start.3
  90.8 46.5 %collective-permute-done.3 = bf16[4,4,96,512]{3,2,1,0:T(8,128)(2,1)S(1)} collective-permute-done((bf16[4,4,96,512]{3,2,1,0:T(8,128)(2,1)}, bf16[4,4,96,512]{3,2,1,0:T(8,128)(2,1)S(1)}, u32[]{:S(2)}, u32[]{:S(2)}) %collective-permute-start.3) | collective-permute-done | bytes 1572896 | tf_op jit(solution)/shard_map/ppermute | solution.py:225
  137.3 3.4 %pad_maximum_fusion.refs_0_ = bf16[8,4,96,512]{3,2,1,0:T(8,128)(2,1)} fusion(bf16[4,4,96,512]{3,2,1,0:T(8,128)(2,1)S(1)} %collective-permute-done.3, bf16[4,4,96,512]{3,2,1,0:T(8,128)(2,1)} %tie.9), kind=kLoop, calls=%fused_computation | loop fusion | flops 1572864 | bytes 6291456 | tf_op jit(solution)/shard_map/concatenate | solution.py:325
  140.7 0.0 all-to-all-done.2
  140.7 0.0 copy-start.3
  140.7 1.1 copy-done.3
  141.7 0.0 collective-permute-start.4
  141.7 0.0 copy-start.7
  141.7 4.9 %all-to-all-start.3 = ((bf16[16,256,128]{2,1,0:T(8,128)(2,1)}), bf16[16,256,128]{2,1,0:T(8,128)(2,1)S(1)}, u32[]{:S(2)}, u32[]{:S(2)}) async-start(bf16[16,256,128]{2,1,0:T(8,128)(2,1)} %tie.11), calls=%async_computation.3 | async-start | bytes 2097152 | tf_op jit(solution)/shard_map/all_to_all | solution.py:319
  146.6 0.0 copy-done.7
  146.6 0.1 copy.23
  146.7 1.6 collective-permute-start
  150.2 5.2 %collective-permute-done = bf16[30,8,512]{2,0,1:T(8,128)(2,1)S(1)} collective-permute-done((bf16[30,8,512]{2,0,1:T(8,128)(2,1)S(1)}, bf16[30,8,512]{2,0,1:T(8,128)(2,1)S(1)}, u32[]{:S(2)}, u32[]{:S(2)}) %collective-permute-start) | collective-permute-done | bytes 245792 | tf_op jit(solution)/shard_map/ppermute | solution.py:248
  155.4 0.6 fusion.carried_ref
  156.1 0.0 collective-permute-done.4.refs_3_.refs_4_
  156.1 13.2 %stage.2 = (bf16[1024,512]{1,0:T(8,128)(2,1)}, f32[30,512]{1,0:T(8,128)}) custom-call(s32[8,1024]{1,0:T(8,128)} %copy-done, s32[1]{0:T(128)} %bitcast.4.me_ref, f32[8,1024]{1,0:T(8,128)} %bitcast.53, f32[30,512]{1,0:T(8,128)} %fusion.carried_ref, f32[4,512]{1,0:T(4,128)} %gain_ref.3, bf16[3072,128]{1,0:T(8,128)(2,1)} %bitcast.45, ...), custom_call_target="tpu_custom_call" | custom-call | flops 3221225472 | bytes 25165824 | tf_op jit(solution)/shard_map/stage/pallas_call | solution.py:341
  169.3 0.2 all-to-all-done.3
  169.6 0.0 copy-start.6
  169.6 1.1 copy-done.6
  170.6 13.8 %stage.3 = (bf16[1024,512]{1,0:T(8,128)(2,1)}, f32[30,512]{1,0:T(8,128)}) custom-call(s32[8,1024]{1,0:T(8,128)} %copy-done, s32[1]{0:T(128)} %bitcast.4.me_ref, f32[8,1024]{1,0:T(8,128)} %bitcast.54, f32[30,512]{1,0:T(8,128)} %get-tuple-element.12.carried_ref, f32[4,512]{1,0:T(4,128)} %gain_ref.3, ...), custom_call_target="tpu_custom_call", output_to_operand_aliasing={{0}: (10, {})} | custom-call | flops 3221225472 | bytes 25165824 | tf_op jit(solution)/shard_map/stage/pallas_call | solution.py:341
  (6 shorter events, 0.0 us)
Async XLA Ops:
  1.8 0.8 copy-start.1
  2.5 0.8 copy-start.2
  4.5 14.1 %copy-start = (s32[8,1024]{1,0:T(8,128)}, s32[8,1024]{1,0:T(8,128)S(1)}, u32[]{:S(2)}) copy-start(s32[8,1024]{1,0:T(8,128)S(1)} %get-tuple-element.10.refs_1_.place_ref) | copy-start | bytes 98308
  24.0 57.0 %all-to-all-start.1 = ((bf16[16,192,128]{2,1,0:T(8,128)(2,1)}), bf16[16,192,128]{2,1,0:T(8,128)(2,1)S(1)}, u32[]{:S(2)}, u32[]{:S(2)}) async-start(bf16[16,192,128]{2,1,0:T(8,128)(2,1)} %owner_gather.3.refs_0_.refs_1_), calls=%async_computation.1 | async-start | bytes 1572864 | tf_op jit(solution)/shard_map/all_to_all | solution.py:319
  27.7 37.7 %collective-permute-start.1 = (bf16[1,4,96,512]{3,2,1,0:T(8,128)(2,1)}, bf16[1,4,96,512]{3,2,1,0:T(8,128)(2,1)S(1)}, u32[]{:S(2)}, u32[]{:S(2)}) collective-permute-start(bf16[1,4,96,512]{3,2,1,0:T(8,128)(2,1)} %tie.7), channel_id=1, source_target_pairs={{0,16},{2,18},{4,20},{6,22},{8,24},{10,26},{12,28},{14,30},{16,0},... | collective-permute-start | bytes 1179656 | tf_op jit(solution)/shard_map/ppermute | solution.py:225
  67.3 19.4 %collective-permute-start.2 = (bf16[2,4,96,512]{3,2,1,0:T(8,128)(2,1)}, bf16[2,4,96,512]{3,2,1,0:T(8,128)(2,1)}, u32[]{:S(2)}, u32[]{:S(2)}) collective-permute-start(bf16[2,4,96,512]{3,2,1,0:T(8,128)(2,1)} %tie.8), channel_id=1, source_target_pairs={{0,8},{2,10},{4,12},{6,14},{8,0},{10,2},{12,4},{14,6},{16,24},{18,... | collective-permute-start | bytes 2359304 | tf_op jit(solution)/shard_map/ppermute | solution.py:225
  81.0 0.9 copy-start.5
  82.0 4.7 %copy-start.4 = (bf16[2,4,96,512]{3,2,1,0:T(8,128)(2,1)S(1)}, bf16[2,4,96,512]{3,2,1,0:T(8,128)(2,1)}, u32[]{:S(2)}) copy-start(bf16[2,4,96,512]{3,2,1,0:T(8,128)(2,1)} %tie.8) | copy-start | bytes 2359300
  82.0 58.7 %all-to-all-start.2 = ((bf16[16,320,128]{2,1,0:T(8,128)(2,1)}), bf16[16,320,128]{2,1,0:T(8,128)(2,1)S(1)}, u32[]{:S(2)}, u32[]{:S(2)}) async-start(bf16[16,320,128]{2,1,0:T(8,128)(2,1)} %tie.6), calls=%async_computation.2 | async-start | bytes 2621440 | tf_op jit(solution)/shard_map/all_to_all | solution.py:319
  89.1 48.2 %collective-permute-start.3 = (bf16[4,4,96,512]{3,2,1,0:T(8,128)(2,1)}, bf16[4,4,96,512]{3,2,1,0:T(8,128)(2,1)S(1)}, u32[]{:S(2)}, u32[]{:S(2)}) collective-permute-start(bf16[4,4,96,512]{3,2,1,0:T(8,128)(2,1)} %tie.9), channel_id=1, source_target_pairs={{0,4},{2,6},{4,0},{6,2},{8,12},{10,14},{12,8},{14,10},{16,20},{18,... | collective-permute-start | bytes 4718600 | tf_op jit(solution)/shard_map/ppermute | solution.py:225
  140.7 1.1 copy-start.3
  141.7 14.3 %collective-permute-start.4 = (bf16[8,4,96,512]{3,2,1,0:T(8,128)(2,1)}, bf16[8,4,96,512]{3,2,1,0:T(8,128)(2,1)}, u32[]{:S(2)}, u32[]{:S(2)}) collective-permute-start(bf16[8,4,96,512]{3,2,1,0:T(8,128)(2,1)} %tie.10.refs_2_.refs_3_), channel_id=1, source_target_pairs={{0,2},{2,0},{4,6},{6,4},{8,10},{10,8},{12,14},{14,12},{16,18},{18,... | collective-permute-start | bytes 9437192 | tf_op jit(solution)/shard_map/ppermute | solution.py:225
  141.7 4.9 %copy-start.7 = (bf16[8,30,512]{2,0,1:T(8,128)(2,1)S(1)}, bf16[8,30,512]{2,0,1:T(8,128)(2,1)}, u32[]{:S(2)}) copy-start(bf16[8,30,512]{2,0,1:T(8,128)(2,1)} %param.17) | copy-start | bytes 737284
  141.7 27.8 %all-to-all-start.3 = ((bf16[16,256,128]{2,1,0:T(8,128)(2,1)}), bf16[16,256,128]{2,1,0:T(8,128)(2,1)S(1)}, u32[]{:S(2)}, u32[]{:S(2)}) async-start(bf16[16,256,128]{2,1,0:T(8,128)(2,1)} %tie.11), calls=%async_computation.3 | async-start | bytes 2097152 | tf_op jit(solution)/shard_map/all_to_all | solution.py:319
  146.7 8.7 %collective-permute-start = (bf16[30,8,512]{2,0,1:T(8,128)(2,1)S(1)}, bf16[30,8,512]{2,0,1:T(8,128)(2,1)S(1)}, u32[]{:S(2)}, u32[]{:S(2)}) collective-permute-start(bf16[30,8,512]{2,0,1:T(8,128)(2,1)S(1)} %bitcast.52), channel_id=1, source_target_pairs={{0,1},{1,0},{2,3},{3,2},{4,5},{5,4},{6,7},{7,6},{8,9},{9,8},{10,11... | collective-permute-start | bytes 737288 | tf_op jit(solution)/shard_map/ppermute | solution.py:248
  169.6 1.1 copy-start.6

commit v3 on v2

--- a/solution.py
+++ b/solution.py
@@ -131,14 +131,19 @@
     if sources == 1:
         filter_copies.append(pltpu.make_async_copy(filter_refs[0], filters, filter_sems.at[0]))
     else:
-        held, _, depth, _ = filter_refs[0].shape
-        for number in range(2 * held):
-            owner = me_ref[0] ^ shard_offset(2 * held, number)
-            rows = pl.ds(pl.multiple_of(owner * depth, depth), depth)
-            source = filter_refs[number // held].at[number % held]
-            filter_copies.append(
-                pltpu.make_async_copy(source, filters.at[:, rows, :], filter_sems.at[number])
-            )
+        held, half, depth, _ = filter_refs[0].shape
+        for group in range(4):
+            layer = (me_ref[1] ^ (group // 2)) * half
+            for number in range(held):
+                owner = me_ref[0] ^ (shard_offset(held, number) + group % 2)
+                rows = pl.ds(pl.multiple_of(owner * depth, depth), depth)
+                filter_copies.append(
+                    pltpu.make_async_copy(
+                        filter_refs[group].at[number],
+                        filters.at[pl.ds(layer, half), rows, :],
+                        filter_sems.at[group * held + number],
+                    )
+                )
     for copy in filter_copies:
         copy.start()
     start = 0
@@ -218,17 +223,15 @@
         copy.wait()
 
 
-def swap_filters(shards, distance, after):
-    owners = lax.axis_size("table")
-    shards = tie(shards, after)
-    pairs = [(source, source ^ distance) for source in range(owners)]
-    return shards, lax.ppermute(shards, "table", pairs)
-
-
-def shard_offset(owners, number):
+def swapped(array, axis, distance):
+    pairs = [(source, source ^ distance) for source in range(lax.axis_size(axis))]
+    return lax.ppermute(array, axis, pairs)
+
+
+def shard_offset(held, number):
     offset = 0
-    bit = owners // 2
-    while bit:
+    bit = held
+    while bit > 1:
         offset += bit * (number % 2)
         number //= 2
         bit //= 2
@@ -268,7 +271,11 @@
     vmem = pl.BlockSpec(memory_space=pltpu.VMEM)
     anywhere = pl.BlockSpec(memory_space=pl.ANY)
 
-    me = lax.axis_index("table").astype(jnp.int32).reshape(1)
+    me = jnp.stack([lax.axis_index("table"), lax.axis_index("rep") % 2]).astype(jnp.int32)
+    half = conv_weight.shape[0] // 2
+    first_shard = lax.dynamic_slice_in_dim(conv_weight, me[1] * half, half, 0)[None]
+    second_shard = swapped(first_shard, "table", owners // 2)
+    state = carried_rows(returning, home, entry, stores)
     rows_by_slot = bag_rows.reshape(token_count, bag_width).T
     owner_by_slot = bag_owner.reshape(token_count, bag_width).T
     requests, place = pl.pallas_call(
@@ -289,7 +296,9 @@
     sent = []
     for number in range(len(part_ends)):
         piece = cuts[number + 1] - cuts[number]
-        earlier = sent[-1:]
+        earlier = sent[-1:] if sent else [second_shard]
+        if number == 2:
+            earlier = earlier + [state]
         sent.append(
             pl.pallas_call(
                 functools.partial(gather_kernel, capacity, cuts[number]),
@@ -318,19 +327,28 @@
             rows = tie(rows, returned[-1], *sent[number + 1 :])
         arrived = lax.all_to_all(rows, "table", split_axis=0, concat_axis=0, tiled=True)
         returned.append(arrived.reshape(-1, row_width))
-    swaps = owners.bit_length() - 1
-    gates = [place, sent[0]] + [returned[0]] * (swaps - 3) + [returned[1]]
-    filters = [conv_weight[None]]
-    for step in range(swaps):
-        shards = jnp.concatenate(filters, axis=0)
-        filters = list(swap_filters(shards, owners >> (step + 1), gates[step]))
+    shards = jnp.concatenate([first_shard, second_shard], axis=0)
+    distance = owners // 4
+    while distance > 1:
+        shards = tie(shards, sent[0] if distance == owners // 4 else sent[1])
+        shards = jnp.concatenate([shards, swapped(shards, "table", distance)], axis=0)
+        distance //= 2
+    shards = tie(shards, returned[0])
+    others = swapped(shards, "rep", 1)
+    near_shards = swapped(shards, "table", 1)
+    others = tie(others, returned[1])
+    near_others = swapped(others, "table", 1)
+    filters = [shards, near_shards, others, near_others]
     if conv_weight.shape[1] % 16:
-        offsets = [shard_offset(owners, number) for number in range(owners)]
+        offsets = [shard_offset(owners // 2, number) for number in range(owners // 2)]
+        offsets = offsets + [offset + 1 for offset in offsets]
         order = jnp.array([offsets.index(owner) for owner in range(owners)], jnp.int32)
-        sources = order[jnp.arange(owners, dtype=jnp.int32) ^ me]
-        whole = jnp.concatenate(filters, axis=0)[sources]
-        filters = [whole.transpose(1, 0, 2, 3).reshape(conv_weight.shape[0], -1, channels)]
-    state = carried_rows(returning, home, entry, stores)
+        sources = order[jnp.arange(owners, dtype=jnp.int32) ^ me[0]]
+        mine = jnp.concatenate(filters[:2], axis=0)[sources]
+        rest = jnp.concatenate(filters[2:], axis=0)[sources]
+        low, high = jnp.where(me[1] == 0, mine, rest), jnp.where(me[1] == 0, rest, mine)
+        whole = jnp.concatenate([low, high], axis=1).transpose(1, 0, 2, 3)
+        filters = [whole.reshape(conv_weight.shape[0], -1, channels)]
     weight_by_slot = bag_weight.reshape(token_count, bag_width).T
     hidden = None
     for number, part in enumerate(stage_parts):
@@ -355,7 +373,7 @@
                 pltpu.VMEM((slots + 16, channels), jnp.float32),
                 pltpu.VMEM((slots + 16, channels), jnp.float32),
                 pltpu.VMEM((slots, channels), jnp.bfloat16),
-                pltpu.SemaphoreType.DMA((owners,)),
+                pltpu.SemaphoreType.DMA((2 * owners,)),
                 pltpu.SemaphoreType.DMA(((slots + 255) // 256,)),
             ],
             input_output_aliases={5 + part + len(filters): 0} if known else {},

time: 187 us -> 164 us (0.88)
  waiting for transfers between devices: 87.1 us -> 63.4 us
  starting transfers between devices: 19 us -> 23.8 us
  local copies, waits for them, and re-layouts: 6.45 us -> 10.1 us
  blocking collectives: 14.1 us -> 10.6 us
  other arithmetic: 8.38 us -> 5.44 us
    ppermute x4 -> x6, waiting for transfers between devices: 81.7 us -> 63.4 us  [swapped(): return lax.ppermute(array, axis, pairs)]
    ppermute x1, waiting for transfers between devices: 5.18 us -> 0.01 us  [carried_rows(): arrived = lax.ppermute(by_position, 'rep', pairs)]
    ppermute x4 -> x6, starting transfers between devices: 4.48 us -> 8.79 us  [swapped(): return lax.ppermute(array, axis, pairs)]
    unnamed x18 -> x28, local copies, waits for them, and re-layouts: 6.45 us -> 10.1 us
    concatenate x3, other arithmetic: 7.75 us -> 4.19 us  [the longest x2 3.4 us: local(): jnp.concatenate([shards, swapped(shards, 'table', distance)], axis=0)]
    all_to_all x1, blocking collectives: 14.1 us -> 10.6 us  [local(): lax.all_to_all(requests, 'table', split_axis=0, concat_axis=0, tiled=True)]
  transfers between devices with their start and end apart: 8 -> 10, of which waited for: 5 -> 3; matrix products, arithmetic and copies ran while one was open for 5% -> 5% of each run, Pallas kernels for 15% -> 17%
where the time goes in v3:
time: 164 us; the launch traced here: 163 us
  waiting for transfers between devices  63.4 us (39%)
  Pallas kernels  47.8 us (29%)
  starting transfers between devices  23.8 us (15%)
  blocking collectives  10.6 us (6%)
  local copies, waits for them, and re-layouts  10.1 us (6%)
  other arithmetic  5.44 us (3%)
  between operations  2.3 us (1%)
    ppermute x6, waiting for transfers between devices, swapped(): return lax.ppermute(array, axis, pairs)  63.4 us
    pallas_call x2, Pallas kernels, local(): pl.pallas_call(functools.partial(stage_kernel, part, len(filters), first,...  27.5 us
    pallas_call x3, Pallas kernels, local(): pl.pallas_call(functools.partial(gather_kernel, capacity, cuts[number]),...  19.1 us
    all_to_all x3, starting transfers between devices, local(): lax.all_to_all(rows, 'table', split_axis=0, concat_axis=0, tiled=True)  13.4 us
    all_to_all x1, blocking collectives, local(): lax.all_to_all(requests, 'table', split_axis=0, concat_axis=0, tiled=True)  10.6 us
    unnamed x28, local copies, waits for them, and re-layouts  10.1 us
    ppermute x6, starting transfers between devices, swapped(): return lax.ppermute(array, axis, pairs)  8.79 us
    concatenate x2, other arithmetic, local(): jnp.concatenate([shards, swapped(shards, 'table', distance)], axis=0)  3.4 us
  transfers between devices with their start and end apart: 10, of which 3 were waited for; matrix products, arithmetic and copies ran while one was open for 5% of the time, Pallas kernels for 17%

profile of v3, /device:TPU:0, one launch (start us, length us, event | category | flops | bytes accessed | tf_op | source)
XLA Modules:
  0.0 163.5 jit_solution(6552713192184360385)
XLA Ops:
  0.0 0.0 copy-start
  0.0 1.0 copy-done
  1.0 4.1 %collective-permute-start.1 = (bf16[1,2,96,512]{3,2,1,0:T(8,128)(2,1)S(1)}, bf16[1,2,96,512]{3,2,1,0:T(8,128)(2,1)S(1)}, u32[]{:S(2)}, u32[]{:S(2)}) collective-permute-start(bf16[1,2,96,512]{3,2,1,0:T(8,128)(2,1)S(1)} %dynamic-slice_bitcast_fusion), channel_id=1, source_target_pairs={{0,16},{2,18},{4,20},{6,22},{8,24},{10,26},{12,28},{14,30},{16,0},... | collective-permute-start | bytes 589832 | tf_op jit(solution)/shard_map/ppermute | solution.py:228
  5.1 0.8 copy-done.1
  5.9 0.8 copy-done.2
  6.6 1.2 prep.1
  7.9 0.0 copy-start.3
  7.9 10.6 %all_to_all.20 = s32[16,1,768]{2,1,0:T(1,128)} all-to-all(s32[16,1,768]{2,1,0:T(1,128)S(1)} %get-tuple-element.11), channel_id=1, replica_groups=mesh['table'=16,'rep'=2] {'table'}, dimensions={0} | all-to-all | bytes 98304 | tf_op jit(solution)/shard_map/all_to_all | solution.py:292
  18.5 0.0 copy-done.3
  18.5 0.0 collective-permute-done.1.refs_0_
  18.5 0.7 copy-done.9
  19.2 5.4 %owner_gather.3.refs_0_.refs_1_ = bf16[16,192,128]{2,1,0:T(8,128)(2,1)} custom-call(s32[12288]{0:T(1024)} %bitcast.49, bf16[8192,128]{1,0:T(8,128)(2,1)} %bitcast.38, bf16[1,2,96,512]{3,2,1,0:T(8,128)(2,1)} %copy-done.9), custom_call_target="tpu_custom_call" | custom-call | bytes 20971520 | tf_op jit(solution)/shard_map/owner_gather/pallas_call | solution.py:303
  24.6 0.0 copy-start.10
  24.6 0.0 copy-start.11
  24.6 3.8 %all-to-all-start.1 = ((bf16[16,192,128]{2,1,0:T(8,128)(2,1)}), bf16[16,192,128]{2,1,0:T(8,128)(2,1)S(1)}, u32[]{:S(2)}, u32[]{:S(2)}) async-start(bf16[16,192,128]{2,1,0:T(8,128)(2,1)} %owner_gather.3.refs_0_.refs_1_), calls=%async_computation.1 | async-start | bytes 1572864 | tf_op jit(solution)/shard_map/all_to_all | solution.py:328
  28.4 0.8 pad_maximum_fusion.2.refs_0_
  29.2 1.8 %collective-permute-start.2 = (bf16[2,2,96,512]{3,2,1,0:T(8,128)(2,1)}, bf16[2,2,96,512]{3,2,1,0:T(8,128)(2,1)S(1)}, u32[]{:S(2)}, u32[]{:S(2)}) collective-permute-start(bf16[2,2,96,512]{3,2,1,0:T(8,128)(2,1)} %tie.7), channel_id=1, source_target_pairs={{0,8},{2,10},{4,12},{6,14},{8,0},{10,2},{12,4},{14,6},{16,24},{18,... | collective-permute-start | bytes 1179656 | tf_op jit(solution)/shard_map/ppermute | solution.py:228
  31.0 0.1 copy.23
  31.1 1.6 collective-permute-start
  34.6 7.3 %owner_gather.4.refs_0_.refs_1_ = bf16[16,320,128]{2,1,0:T(8,128)(2,1)} custom-call(s32[12288]{0:T(1024)} %bitcast.50, bf16[8192,128]{1,0:T(8,128)(2,1)} %bitcast.39, bf16[16,192,128]{2,1,0:T(8,128)(2,1)} %owner_gather.3.refs_0_.refs_1_), custom_call_target="tpu_custom_call" | custom-call | bytes 20971520 | tf_op jit(solution)/shard_map/owner_gather/pallas_call | solution.py:303
  41.9 2.5 %copy.24.refs_0_ = bf16[16,320,128]{2,1,0:T(8,128)(2,1)} copy(bf16[16,320,128]{2,1,0:T(8,128)(2,1)} %owner_gather.4.refs_0_.refs_1_) | data formatting | bytes 2621440
  44.4 0.0 collective-permute-done
  44.4 0.6 fusion.refs_1_.carried_ref
  45.1 6.4 %owner_gather.5.refs_2_.refs_0_ = bf16[16,256,128]{2,1,0:T(8,128)(2,1)} custom-call(s32[12288]{0:T(1024)} %bitcast.51, bf16[8192,128]{1,0:T(8,128)(2,1)} %bitcast.40, bf16[16,320,128]{2,1,0:T(8,128)(2,1)} %owner_gather.4.refs_0_.refs_1_, f32[30,512]{1,0:T(8,128)} %fusion.refs_1_.carried_ref), custom_call_target="tpu_custom_call" | custom-call | bytes 20971520 | tf_op jit(solution)/shard_map/owner_gather/pallas_call | solution.py:303
  51.4 0.0 all-to-all-done.1
  51.4 0.0 copy-start.5
  51.4 0.9 copy-done.5
  52.3 4.8 %all-to-all-start.2 = ((bf16[16,320,128]{2,1,0:T(8,128)(2,1)}), bf16[16,320,128]{2,1,0:T(8,128)(2,1)S(1)}, u32[]{:S(2)}, u32[]{:S(2)}) async-start(bf16[16,320,128]{2,1,0:T(8,128)(2,1)} %tie.6), calls=%async_computation.2 | async-start | bytes 2621440 | tf_op jit(solution)/shard_map/all_to_all | solution.py:328
  57.2 0.0 collective-permute-done.2
  57.2 0.9 pad_maximum_fusion.1.refs_0_
  58.1 1.9 %collective-permute-start.3 = (bf16[4,2,96,512]{3,2,1,0:T(8,128)(2,1)}, bf16[4,2,96,512]{3,2,1,0:T(8,128)(2,1)S(1)}, u32[]{:S(2)}, u32[]{:S(2)}) collective-permute-start(bf16[4,2,96,512]{3,2,1,0:T(8,128)(2,1)} %tie.8), channel_id=1, source_target_pairs={{0,4},{2,6},{4,0},{6,2},{8,12},{10,14},{12,8},{14,10},{16,20},{18,... | collective-permute-start | bytes 2359304 | tf_op jit(solution)/shard_map/ppermute | solution.py:228
  60.1 31.1 %collective-permute-done.3 = bf16[4,2,96,512]{3,2,1,0:T(8,128)(2,1)S(1)} collective-permute-done((bf16[4,2,96,512]{3,2,1,0:T(8,128)(2,1)}, bf16[4,2,96,512]{3,2,1,0:T(8,128)(2,1)S(1)}, u32[]{:S(2)}, u32[]{:S(2)}) %collective-permute-start.3) | collective-permute-done | bytes 786464 | tf_op jit(solution)/shard_map/ppermute | solution.py:228
  91.2 2.5 %pad_maximum_fusion.refs_0_ = bf16[8,2,96,512]{3,2,1,0:T(8,128)(2,1)} fusion(bf16[4,2,96,512]{3,2,1,0:T(8,128)(2,1)S(1)} %collective-permute-done.3, bf16[4,2,96,512]{3,2,1,0:T(8,128)(2,1)} %tie.8), kind=kLoop, calls=%fused_computation | loop fusion | flops 786432 | bytes 3145728 | tf_op jit(solution)/shard_map/concatenate | solution.py:334
  93.7 0.5 collective-permute-start.5
  94.2 0.0 all-to-all-done.2
  94.2 1.1 copy-done.4
  95.3 4.8 %all-to-all-start.3 = ((bf16[16,256,128]{2,1,0:T(8,128)(2,1)}), bf16[16,256,128]{2,1,0:T(8,128)(2,1)}, u32[]{:S(2)}, u32[]{:S(2)}) async-start(bf16[16,256,128]{2,1,0:T(8,128)(2,1)} %tie.11), calls=%async_computation.3 | async-start | bytes 2097152 | tf_op jit(solution)/shard_map/all_to_all | solution.py:328
  100.1 0.4 collective-permute-start.4
  100.5 29.3 %collective-permute-done.5.refs_0_ = bf16[8,2,96,512]{3,2,1,0:T(8,128)(2,1)S(1)} collective-permute-done((bf16[8,2,96,512]{3,2,1,0:T(8,128)(2,1)}, bf16[8,2,96,512]{3,2,1,0:T(8,128)(2,1)S(1)}, u32[]{:S(2)}, u32[]{:S(2)}) %collective-permute-start.5) | collective-permute-done | bytes 1572896 | tf_op jit(solution)/shard_map/ppermute | solution.py:228
  129.8 1.2 copy-done.8
  131.0 0.0 collective-permute-start.6
  131.0 0.6 pad_add_fusion.me_ref
  131.6 0.0 collective-permute-done.4.refs_3_.refs_4_
  131.6 3.0 %collective-permute-done.6.refs_5_.refs_6_ = bf16[8,2,96,512]{3,2,1,0:T(8,128)(2,1)S(1)} collective-permute-done((bf16[8,2,96,512]{3,2,1,0:T(8,128)(2,1)}, bf16[8,2,96,512]{3,2,1,0:T(8,128)(2,1)S(1)}, u32[]{:S(2)}, u32[]{:S(2)}) %collective-permute-start.6) | collective-permute-done | bytes 1572896 | tf_op jit(solution)/shard_map/ppermute | solution.py:228
  134.6 1.1 copy-done.12
  135.8 13.5 %stage.2 = (bf16[1024,512]{1,0:T(8,128)(2,1)}, f32[30,512]{1,0:T(8,128)}) custom-call(s32[8,1024]{1,0:T(8,128)} %copy-done.3, s32[2]{0:T(128)} %pad_add_fusion.me_ref, f32[8,1024]{1,0:T(8,128)} %bitcast.53, f32[30,512]{1,0:T(8,128)} %fusion.refs_1_.carried_ref, f32[4,512]{1,0:T(4,128)} %gain_ref.3, bf16[3072,128]{1,0:T(8,128)(2,1)} %bitcast.47, ...), custom_call_target="tpu_custom_call" | custom-call | flops 3221225472 | bytes 25165824 | tf_op jit(solution)/shard_map/stage/pallas_call | solution.py:359
  149.2 0.0 all-to-all-done.3
  149.2 14.0 %stage.3 = (bf16[1024,512]{1,0:T(8,128)(2,1)}, f32[30,512]{1,0:T(8,128)}) custom-call(s32[8,1024]{1,0:T(8,128)} %copy-done.3, s32[2]{0:T(128)} %pad_add_fusion.me_ref, f32[8,1024]{1,0:T(8,128)} %bitcast.54, f32[30,512]{1,0:T(8,128)} %get-tuple-element.12.carried_ref, f32[4,512]{1,0:T(4,128)} %gain_ref.3, ...), custom_call_target="tpu_custom_call", output_to_operand_aliasing={{0}: (12, {})} | custom-call | flops 3221225472 | bytes 25165824 | tf_op jit(solution)/shard_map/stage/pallas_call | solution.py:359
  (19 shorter events, 0.0 us)
Async XLA Ops:
  0.0 1.0 copy-start
  1.0 17.5 %collective-permute-start.1 = (bf16[1,2,96,512]{3,2,1,0:T(8,128)(2,1)S(1)}, bf16[1,2,96,512]{3,2,1,0:T(8,128)(2,1)S(1)}, u32[]{:S(2)}, u32[]{:S(2)}) collective-permute-start(bf16[1,2,96,512]{3,2,1,0:T(8,128)(2,1)S(1)} %dynamic-slice_bitcast_fusion), channel_id=1, source_target_pairs={{0,16},{2,18},{4,20},{6,22},{8,24},{10,26},{12,28},{14,30},{16,0},... | collective-permute-start | bytes 589832 | tf_op jit(solution)/shard_map/ppermute | solution.py:228
  5.1 0.8 copy-start.1
  5.9 0.8 copy-start.2
  7.9 10.6 %copy-start.3 = (s32[8,1024]{1,0:T(8,128)}, s32[8,1024]{1,0:T(8,128)S(1)}, u32[]{:S(2)}) copy-start(s32[8,1024]{1,0:T(8,128)S(1)} %get-tuple-element.10.place_ref) | copy-start | bytes 98308
  18.5 0.7 copy-start.9
  24.6 3.8 %copy-start.10 = (bf16[1,2,96,512]{3,2,1,0:T(8,128)(2,1)S(1)}, bf16[1,2,96,512]{3,2,1,0:T(8,128)(2,1)}, u32[]{:S(2)}) copy-start(bf16[1,2,96,512]{3,2,1,0:T(8,128)(2,1)} %copy-done.9) | copy-start | bytes 589828
  24.6 6.4 %copy-start.11 = (bf16[8,30,512]{2,0,1:T(8,128)(2,1)S(1)}, bf16[8,30,512]{2,0,1:T(8,128)(2,1)}, u32[]{:S(2)}) copy-start(bf16[8,30,512]{2,0,1:T(8,128)(2,1)} %param.17) | copy-start | bytes 737284
  24.6 26.8 %all-to-all-start.1 = ((bf16[16,192,128]{2,1,0:T(8,128)(2,1)}), bf16[16,192,128]{2,1,0:T(8,128)(2,1)S(1)}, u32[]{:S(2)}, u32[]{:S(2)}) async-start(bf16[16,192,128]{2,1,0:T(8,128)(2,1)} %owner_gather.3.refs_0_.refs_1_), calls=%async_computation.1 | async-start | bytes 1572864 | tf_op jit(solution)/shard_map/all_to_all | solution.py:328
  29.2 28.0 %collective-permute-start.2 = (bf16[2,2,96,512]{3,2,1,0:T(8,128)(2,1)}, bf16[2,2,96,512]{3,2,1,0:T(8,128)(2,1)S(1)}, u32[]{:S(2)}, u32[]{:S(2)}) collective-permute-start(bf16[2,2,96,512]{3,2,1,0:T(8,128)(2,1)} %tie.7), channel_id=1, source_target_pairs={{0,8},{2,10},{4,12},{6,14},{8,0},{10,2},{12,4},{14,6},{16,24},{18,... | collective-permute-start | bytes 1179656 | tf_op jit(solution)/shard_map/ppermute | solution.py:228
  31.1 13.3 %collective-permute-start = (bf16[30,8,512]{2,0,1:T(8,128)(2,1)S(1)}, bf16[30,8,512]{2,0,1:T(8,128)(2,1)S(1)}, u32[]{:S(2)}, u32[]{:S(2)}) collective-permute-start(bf16[30,8,512]{2,0,1:T(8,128)(2,1)S(1)} %bitcast.52), channel_id=1, source_target_pairs={{0,1},{1,0},{2,3},{3,2},{4,5},{5,4},{6,7},{7,6},{8,9},{9,8},{10,11... | collective-permute-start | bytes 737288 | tf_op jit(solution)/shard_map/ppermute | solution.py:251
  51.4 0.9 copy-start.5
  52.3 4.9 %copy-start.7 = (bf16[2,2,96,512]{3,2,1,0:T(8,128)(2,1)S(1)}, bf16[2,2,96,512]{3,2,1,0:T(8,128)(2,1)}, u32[]{:S(2)}) copy-start(bf16[2,2,96,512]{3,2,1,0:T(8,128)(2,1)} %tie.7) | copy-start | bytes 1179652
  52.3 41.9 %all-to-all-start.2 = ((bf16[16,320,128]{2,1,0:T(8,128)(2,1)}), bf16[16,320,128]{2,1,0:T(8,128)(2,1)S(1)}, u32[]{:S(2)}, u32[]{:S(2)}) async-start(bf16[16,320,128]{2,1,0:T(8,128)(2,1)} %tie.6), calls=%async_computation.2 | async-start | bytes 2621440 | tf_op jit(solution)/shard_map/all_to_all | solution.py:328
  58.1 33.1 %collective-permute-start.3 = (bf16[4,2,96,512]{3,2,1,0:T(8,128)(2,1)}, bf16[4,2,96,512]{3,2,1,0:T(8,128)(2,1)S(1)}, u32[]{:S(2)}, u32[]{:S(2)}) collective-permute-start(bf16[4,2,96,512]{3,2,1,0:T(8,128)(2,1)} %tie.8), channel_id=1, source_target_pairs={{0,4},{2,6},{4,0},{6,2},{8,12},{10,14},{12,8},{14,10},{16,20},{18,... | collective-permute-start | bytes 2359304 | tf_op jit(solution)/shard_map/ppermute | solution.py:228
  93.7 36.1 %collective-permute-start.5 = (bf16[8,2,96,512]{3,2,1,0:T(8,128)(2,1)}, bf16[8,2,96,512]{3,2,1,0:T(8,128)(2,1)S(1)}, u32[]{:S(2)}, u32[]{:S(2)}) collective-permute-start(bf16[8,2,96,512]{3,2,1,0:T(8,128)(2,1)} %tie.9.refs_2_.refs_3_), channel_id=1, source_target_pairs={{0,1},{1,0},{2,3},{3,2},{4,5},{5,4},{6,7},{7,6},{8,9},{9,8},{10,11... | collective-permute-start | bytes 4718600 | tf_op jit(solution)/shard_map/ppermute | solution.py:228
  94.2 1.1 copy-start.4
  95.3 4.9 %copy-start.6 = (bf16[8,2,96,512]{3,2,1,0:T(8,128)(2,1)S(1)}, bf16[8,2,96,512]{3,2,1,0:T(8,128)(2,1)}, u32[]{:S(2)}) copy-start(bf16[8,2,96,512]{3,2,1,0:T(8,128)(2,1)} %tie.9.refs_2_.refs_3_) | copy-start | bytes 4718596
  95.3 54.0 %all-to-all-start.3 = ((bf16[16,256,128]{2,1,0:T(8,128)(2,1)}), bf16[16,256,128]{2,1,0:T(8,128)(2,1)}, u32[]{:S(2)}, u32[]{:S(2)}) async-start(bf16[16,256,128]{2,1,0:T(8,128)(2,1)} %tie.11), calls=%async_computation.3 | async-start | bytes 2097152 | tf_op jit(solution)/shard_map/all_to_all | solution.py:328
  100.1 31.5 %collective-permute-start.4 = (bf16[8,2,96,512]{3,2,1,0:T(8,128)(2,1)S(1)}, bf16[8,2,96,512]{3,2,1,0:T(8,128)(2,1)}, u32[]{:S(2)}, u32[]{:S(2)}) collective-permute-start(bf16[8,2,96,512]{3,2,1,0:T(8,128)(2,1)S(1)} %copy-done.6), channel_id=1, source_target_pairs={{0,2},{2,0},{4,6},{6,4},{8,10},{10,8},{12,14},{14,12},{16,18},{18,... | collective-permute-start | bytes 4718600 | tf_op jit(solution)/shard_map/ppermute | solution.py:228
  129.8 1.2 copy-start.8
  131.0 3.6 %collective-permute-start.6 = (bf16[8,2,96,512]{3,2,1,0:T(8,128)(2,1)}, bf16[8,2,96,512]{3,2,1,0:T(8,128)(2,1)S(1)}, u32[]{:S(2)}, u32[]{:S(2)}) collective-permute-start(bf16[8,2,96,512]{3,2,1,0:T(8,128)(2,1)} %tie.10.refs_4_.refs_5_), channel_id=1, source_target_pairs={{0,2},{2,0},{4,6},{6,4},{8,10},{10,8},{12,14},{14,12},{16,18},{18,... | collective-permute-start | bytes 4718600 | tf_op jit(solution)/shard_map/ppermute | solution.py:228
  134.6 1.1 copy-start.12
